TPU v7x, 32 devices: a whole 2x2x4 slice. The times are simulated.
32 devices in a mesh: tile: 16 (over z, y, x), scene: 2 (over core).
Axes of the slice: x: 2, y: 2, z: 4, core: 2. Of those that a mesh axis runs over, the one named last changes fastest.
Arguments:
- points: bfloat16 [2, 2, 9, 32, 2048], P(None, 'scene', None, None, 'tile'), may hold values from -6 to 6
- point_counts: int32 [2, 2, 2048], P(None, 'scene', 'tile'), may hold values from 1 to 32, as said below
- pillar_tile: int32 [2, 2, 2048], P(None, 'scene', 'tile'), may hold values from 0 to 15, as said below
- pillar_cell: int32 [2, 2, 2048], P(None, 'scene', 'tile'), may hold values from 0 to 2047
- pillar_weight: bfloat16 [64, 9], P('scene'), may hold values from -2 to 2
- pillar_gain: bfloat16 [64], P('scene'), may hold values from 0.25 to 1.75
- pillar_shift: bfloat16 [64], P('scene'), may hold values from -2.5 to 2.5
- first_weight: bfloat16 [64, 576], P('scene'), may hold values from -0.25 to 0.25
- first_gain: bfloat16 [64], P('scene'), may hold values from 0.25 to 1.75
- first_shift: bfloat16 [64], P('scene'), may hold values from -2.5 to 2.5
- second_weight: bfloat16 [64, 576], P('scene'), may hold values from -0.25 to 0.25
- second_gain: bfloat16 [64], P('scene'), may hold values from 0.25 to 1.75
- second_shift: bfloat16 [64], P('scene'), may hold values from -2.5 to 2.5
- up_weight: bfloat16 [128, 64], P('scene'), may hold values from -0.75 to 0.75
- up_gain: bfloat16 [128], P('scene'), may hold values from 0.25 to 1.75
- up_shift: bfloat16 [128], P('scene'), may hold values from -2.5 to 2.5
- cotangent: bfloat16 [2, 2, 128, 64, 512], P(None, 'scene', None, 'tile'), may hold values from -6 to 6
Outputs:
- features: bfloat16 [2, 2, 128, 64, 512], P(None, 'scene', None, 'tile')
- points_grad: float32 [2, 2, 9, 32, 2048], P(None, 'scene', None, None, 'tile')
- pillar_weight_grad: float32 [64, 9], P('scene')
- pillar_gain_grad: float32 [64], P('scene')
- pillar_shift_grad: float32 [64], P('scene')
- first_weight_grad: float32 [64, 576], P('scene')
- first_gain_grad: float32 [64], P('scene')
- first_shift_grad: float32 [64], P('scene')
- second_weight_grad: float32 [64, 576], P('scene')
- second_gain_grad: float32 [64], P('scene')
- second_shift_grad: float32 [64], P('scene')
- up_weight_grad: float32 [128, 64], P('scene')
- up_gain_grad: float32 [128], P('scene')
- up_shift_grad: float32 [128], P('scene')
Inputs may be any that keep to these rules, and one draw needn't show every extreme that they name: `point_counts`: point slots at or beyond a pillar's count are padding. Each aligned block of 128 pillars holds a pillar of 32 points. `pillar_tile`: each aligned block of 128 pillars names every tile at most 16 times; in each micro-batch and scene one tile is named exactly 16 times by every block.
All inputs are finite; a program needn't handle non-finite values.
Results may differ from a plain program's by a relative error of at most 0.012.
The roundings to bfloat16 on the way count: a program that leaves them out, or rounds other values in their place, can miss the bound.
Values may be sent and summed in bfloat16 or wider, within the bound.
No kernel may reach another device: no remote copies, remote signals or barrier semaphores. Data moves between devices by JAX's collectives and lax.ppermute only.
A program may use at most 128 MiB of HBM per device.

v0:
```python
import functools

import jax
import jax.numpy as jnp
from jax import lax
from jax.experimental import pallas as pl
from jax.experimental.pallas import tpu as pltpu
from jax.sharding import PartitionSpec as P

norm_eps = 0.001
BOTH = ("tile", "scene")
F32 = jnp.float32
BF16 = jnp.bfloat16
VMEM_LIMIT = 24 * 1024 * 1024
WIDE_LIMIT = 60 * 1024 * 1024
LANES = 128


def run(kernel, outs, *args, hbm=(), scratch=(), copies=0, cost=None, limit=VMEM_LIMIT):
    specs = [
        pl.BlockSpec(memory_space=pltpu.HBM if index in hbm else pltpu.VMEM) for index in range(len(args))
    ]
    scratch = list(scratch)
    if copies:
        scratch.append(pltpu.SemaphoreType.DMA((copies,)))
    return pl.pallas_call(
        kernel,
        out_shape=[jax.ShapeDtypeStruct(out[0], out[1]) for out in outs],
        in_specs=specs,
        out_specs=[
            pl.BlockSpec(memory_space=pltpu.HBM if len(out) > 2 else pltpu.VMEM) for out in outs
        ],
        scratch_shapes=scratch,
        compiler_params=pltpu.CompilerParams(vmem_limit_bytes=limit),
        cost_estimate=cost,
    )(*args)


def move(source, target, sems, index):
    copy = pltpu.make_async_copy(source, target, sems.at[index])
    copy.start()
    return copy


def dot(left, right, precision=None):
    return jnp.dot(left, right, preferred_element_type=F32, precision=precision)


def dot_lanes(left, right, precision=None):
    return lax.dot_general(
        left, right, (((1,), (1,)), ((), ())), preferred_element_type=F32, precision=precision
    )


def sigmoid(values):
    return 0.5 + 0.5 * jnp.tanh(0.5 * values)


def fold(values):
    total = values[:, :LANES]
    for start in range(LANES, values.shape[1], LANES):
        total = total + values[:, start : start + LANES]
    return total


def row_of(left, right=None):
    both = left if right is None else jnp.concatenate([left, right], axis=0)
    return jnp.sum(jnp.transpose(both), axis=0, keepdims=True)


def columns_of(rows):
    rows = rows + [jnp.zeros((8 - len(rows), LANES), F32)] if len(rows) < 8 else rows
    return jnp.transpose(jnp.concatenate(rows, axis=0))


def inside(tile, row, height):
    tiles, rows = height
    place = tile * rows + row
    return jnp.where((place >= 0) & (place < tiles * rows), 1.0, 0.0).astype(F32)


def send_all(ref, rows):
    for index, row in enumerate(rows):
        ref[:, index : index + 1, :] = jnp.broadcast_to(row[None], (ref.shape[0], 1, LANES))


def pooled_stats(means, squares, count):
    peers = means.shape[0]
    mean = jnp.sum(means, axis=0, keepdims=True) * (1.0 / peers)
    away = means - mean
    spread = jnp.sum(squares + count * away * away, axis=0, keepdims=True) * (1.0 / (peers * count))
    return mean, lax.rsqrt(spread + norm_eps)


def stat_columns(found, count):
    return columns_of(list(pooled_stats(found[:, 0, :], found[:, 1, :], count)))


def sum_rows(found, lines):
    return [jnp.sum(found[:, index, :], axis=0, keepdims=True) for index in range(lines)]


def own_half(row, scene, out):
    size = out.shape[0]
    out[...] = jnp.where(scene == 0, row[:, 0:size], row[:, size : 2 * size]).reshape(size)


def edges(channels, width):
    lane = lax.broadcasted_iota(jnp.int32, (channels, width), 1)
    return lane > 0, lane < width - 1


def spread(row, masks):
    zero = jnp.zeros_like(row)
    left = jnp.where(masks[0], pltpu.roll(row, 1, 1), zero)
    right = jnp.where(masks[1], pltpu.roll(row, row.shape[1] - 1, 1), zero)
    return jnp.concatenate([left, row, right], axis=0)


def layout(half, channels):
    first = 0
    second = first + half * -(-9 * channels // LANES)
    up = second + half * -(-9 * channels // LANES)
    vectors = up + channels
    return first, second, up, vectors, vectors + 16


def widen(value):
    missing = LANES - value.shape[1]
    if missing == 0:
        return value
    return jnp.concatenate([value, jnp.zeros((value.shape[0], missing), value.dtype)], axis=1)


def pack(held, out):
    first, second, up, pillar = held[:4]
    half, channels = first.shape[0], up.shape[1]
    starts = layout(half, channels)
    for ref, start in ((first, starts[0]), (second, starts[1])):
        for j in range(-(-9 * channels // LANES)):
            out[start + j * half : start + (j + 1) * half, :] = widen(
                ref[:, j * LANES : min((j + 1) * LANES, 9 * channels)]
            )
    out[starts[2] : starts[2] + channels, :] = widen(up[...])
    rows = [vector[...].astype(F32).reshape(1, -1) for vector in held[4:]]
    rows = [widen(row) for row in rows] + [jnp.zeros((16 - len(rows), LANES), F32)]
    turned = widen(pillar[...].astype(F32))
    rows += [turned, jnp.zeros((16 - turned.shape[0], LANES), F32)]
    out[starts[3] :, :] = jnp.concatenate(rows, axis=0).astype(BF16)


def unpack_kernel(
    both, w_pillar, cols, l_first, l_second, b_first, b_second, w_up, w_up_t, *, inputs
):
    half = w_pillar.shape[0] // 2
    channels = 2 * half
    starts = layout(half, channels)
    tiles = -(-9 * channels // LANES)

    def wide(start):
        return jnp.concatenate(
            [
                jnp.concatenate(
                    [both[s, start + j * half : start + (j + 1) * half, :] for j in range(tiles)], axis=1
                )
                for s in range(2)
            ],
            axis=0,
        ).astype(F32)

    up = jnp.concatenate(
        [both[s, starts[2] : starts[2] + channels, 0:channels] for s in range(2)], axis=0
    )
    w_up[...] = up
    w_up_t[...] = jnp.transpose(up.astype(F32)).astype(BF16)
    turned = jnp.concatenate(
        [both[s, starts[4] : starts[4] + 16, 0:half].astype(F32) for s in range(2)], axis=1
    )
    w_pillar[...] = jnp.transpose(widen(turned))[0:channels, 0:inputs].astype(BF16)
    vectors = [both[s, starts[3] : starts[3] + 16, :].astype(F32) for s in range(2)]
    rows = []
    for index in range(8):
        size = half if index < 6 else channels
        row = jnp.concatenate([vectors[s][index : index + 1, 0:size] for s in range(2)], axis=1)
        rows.append(jnp.concatenate([row] * (LANES // (2 * size)), axis=1))
    cols[...] = columns_of(rows)
    for weight, ahead, back in ((wide(starts[0]), l_first, b_first), (wide(starts[1]), l_second, b_second)):
        turned = jnp.transpose(weight)
        ahead[...] = weight[:, : 9 * channels].astype(BF16)
        back[...] = jnp.concatenate(
            [turned[tap * channels : (tap + 1) * channels] for tap in range(8, -1, -1)], axis=1
        ).astype(BF16)


def slot_line(wide, depth, inputs):
    return jnp.concatenate([wide[pl.ds(n, inputs, stride=depth), :] for n in range(depth)], axis=1)


def slot_mask(count, depth):
    return jnp.concatenate([jnp.where(count > n, 1.0, 0.0) for n in range(depth)], axis=1)


def ranks(tile):
    pillars = tile.shape[1]
    across = jnp.broadcast_to(tile, (pillars, pillars))
    down = jnp.transpose(across)
    row = lax.broadcasted_iota(jnp.int32, (pillars, pillars), 0)
    col = lax.broadcasted_iota(jnp.int32, (pillars, pillars), 1)
    return jnp.sum(jnp.where((across == down) & (row < col), 1.0, 0.0), axis=0, keepdims=True)


def moments_kernel(*refs, capacity):
    number = 4
    sources, out = refs[:number], refs[number]
    held, wide, sems = refs[number + 1 : 2 * number + 1], refs[-2], refs[-1]
    copies = [move(sources[i], held[i], sems, i) for i in range(number)]
    tiles, cells, counts, points = held
    micros, _, inputs, depth, pillars = points.shape
    peers, scenes = out.shape[:2]
    copies[0].wait()
    copies[1].wait()
    lines = []
    for micro in range(micros):
        tile = tiles[micro].astype(F32)
        cell = (cells[micro] + 1).astype(F32)
        high = jnp.floor(cell * (1.0 / 16.0))
        low = cell - high * 16.0
        rank = ranks(tile)
        spot = lax.broadcasted_iota(jnp.int32, (capacity, pillars), 0).astype(F32)
        placed = jnp.where(spot == rank, 1.0, 0.0).astype(BF16)
        peer = lax.broadcasted_iota(jnp.int32, (peers, pillars), 0).astype(F32)
        for group in range(3):
            named = tile == peer + (group - 1.0)
            lines.append(
                16.0 * dot_lanes(jnp.where(named, high, 0.0).astype(BF16), placed)
                + dot_lanes(jnp.where(named, low, 0.0).astype(BF16), placed)
            )
    used = 3 * micros * capacity
    line = jnp.concatenate(lines + [jnp.zeros((peers, LANES - used), F32)], axis=1).reshape(peers, 1, LANES)
    for scene in range(scenes):
        out[:, scene, micros : micros + 1, :] = line
    copies[2].wait()
    copies[3].wait()
    parts, mean_rows, totals = [], [], []
    for micro in range(micros):
        wide[...] = points[micro, 0].astype(F32).reshape(inputs * depth, pillars)
        rows = slot_line(wide, depth, inputs)
        mask = slot_mask(counts[micro], depth)
        total = jnp.sum(mask, axis=1, keepdims=True)
        mean = jnp.sum(rows * mask, axis=1, keepdims=True) / total
        centred = jnp.concatenate(
            [(rows - mean) * mask, jnp.zeros((16 - inputs, rows.shape[1]), F32)], axis=0
        )
        high = centred.astype(BF16)
        parts += [high, (centred - high.astype(F32)).astype(BF16)]
        lane = lax.broadcasted_iota(jnp.int32, (inputs, inputs), 1)
        diagonal = lax.broadcasted_iota(jnp.int32, (inputs, inputs), 0) == lane
        mean_rows.append(jnp.sum(jnp.where(diagonal, mean, 0.0), axis=0, keepdims=True))
        totals.append(total)
    parts = jnp.concatenate(parts, axis=0)
    every = dot_lanes(parts, parts)
    for micro in range(micros):
        at = 32 * micro
        square = every[at : at + 32, at : at + 32]
        products = (
            square[0:inputs, 0:inputs] + square[16 : 16 + inputs, 0:inputs]
            + square[0:inputs, 16 : 16 + inputs] + square[16 : 16 + inputs, 16 : 16 + inputs]
        )
        row = jnp.concatenate(
            [products[k : k + 1] for k in range(inputs)]
            + [mean_rows[micro], totals[micro], jnp.zeros((1, LANES - inputs * inputs - inputs - 1), F32)],
            axis=1,
        )
        for scene in range(scenes):
            out[:, scene, micro : micro + 1, :] = jnp.broadcast_to(row[None], (peers, 1, LANES))


def pack_kernel(*refs, capacity):
    number = 15
    sources, packed, lines_out = refs[:number], refs[number], refs[number + 1]
    held, wide, sems = refs[number + 2 : 2 * number + 2], refs[-2], refs[-1]
    copies = [move(sources[i], held[i], sems, i) for i in range(number)]
    for copy in copies:
        copy.wait()
    tiles, counts, points = held[:3]
    pack(held[3:], packed)
    micros, _, inputs, depth, pillars = points.shape
    for micro in range(micros):
        tile = tiles[micro].astype(F32)
        wide[...] = points[micro, 0].astype(F32).reshape(inputs * depth, pillars)
        rows = slot_line(wide, depth, inputs)
        notes = jnp.concatenate([tile * capacity + ranks(tile), counts[micro].astype(F32)], axis=0)
        notes = jnp.concatenate([notes, jnp.zeros((2, rows.shape[1] - pillars), F32)], axis=1)
        lines_out[micro] = jnp.concatenate(
            [rows, notes, jnp.zeros((14 - inputs, rows.shape[1]), F32)], axis=0
        ).astype(BF16)


def cells_kernel(found, rows, *, capacity):
    scene = lax.axis_index("scene")
    slots = rows.shape[1]
    peers = found.shape[0]
    values = found[:, 2, :]
    slot = lax.broadcasted_iota(jnp.int32, (slots, peers), 0)
    peer = lax.broadcasted_iota(jnp.int32, (slots, peers), 1)
    lane = lax.broadcasted_iota(jnp.int32, (slots, LANES), 1)
    row = lax.broadcasted_iota(jnp.int32, (slots, LANES), 0)
    result = jnp.zeros((slots, LANES), F32)
    chosen = jnp.where(peer == 2 * (slot // capacity) + scene, 1.0, 0.0)
    spread = dot(chosen, values, lax.Precision.HIGHEST)
    for micro in range(2):
        for group in range(3):
            mine = jnp.where(lane == (3 * micro + group) * capacity + row % capacity, spread, 0.0)
            column = jnp.sum(mine, axis=1, keepdims=True)
            result = jnp.where(lane == 2 * group + micro, column, result)
    rows[...] = jnp.transpose(result)[0:8]


def pillar_notes(rows, micro, inputs, pillars):
    notes = rows[micro, :, 0:pillars].astype(F32)
    return notes[inputs : inputs + 1], notes[inputs + 1 : inputs + 2]


def pillar_kernel(
    found, point_rows, w_pillar, cols, send, pooled, lifted, acts, *, capacity
):
    micros = point_rows.shape[0]
    channels, inputs = w_pillar.shape
    pillars = pooled.shape[2]
    depth = point_rows.shape[2] // pillars
    weight = w_pillar[...]
    wide_weight = weight.astype(F32)
    rows_out = send.shape[0]
    square = inputs * inputs
    stacked, slot_rows = [], []
    for micro in range(micros):
        lifted[...] = dot(weight, point_rows[micro, 0:inputs])
        moments = found[:, micro, :]
        sizes = moments[:, square + inputs : square + inputs + 1]
        means = moments[:, square : square + inputs]
        count = jnp.sum(sizes, axis=0, keepdims=True)
        mean = jnp.sum(means * sizes, axis=0, keepdims=True) / count
        away = means - mean
        products = lax.dot_general(
            away * sizes, away, (((0,), (0,)), ((), ())),
            preferred_element_type=F32, precision=lax.Precision.HIGHEST,
        )
        summed = jnp.sum(moments, axis=0, keepdims=True)
        products = products + jnp.concatenate(
            [summed[:, k * inputs : (k + 1) * inputs] for k in range(inputs)], axis=0
        )
        cov = products / count
        spun = wide_weight[:, 0:1] * cov[0:1]
        for k in range(1, inputs):
            spun = spun + wide_weight[:, k : k + 1] * cov[k : k + 1]
        spread = jnp.sum(spun * wide_weight, axis=1, keepdims=True)
        centre = jnp.sum(wide_weight * mean, axis=1, keepdims=True)
        rstd = lax.rsqrt(spread + norm_eps)
        inverse = jnp.broadcast_to(1.0 / count, (channels, 1))
        pooled[micros + micro] = jnp.concatenate(
            [
                centre, rstd, inverse, jnp.zeros((channels, 13), F32),
                spun, jnp.zeros((channels, 16 - inputs), F32),
                jnp.broadcast_to(mean, (channels, inputs)), jnp.zeros((channels, LANES - 32 - inputs), F32),
            ],
            axis=1,
        )
        scale = rstd * cols[0:channels, 0:1]
        shift = cols[0:channels, 1:2]
        slot, limit = pillar_notes(point_rows, micro, inputs, pillars)
        slot_rows.append(slot)
        top = jnp.full((channels, pillars), -jnp.inf, F32)
        for n in range(depth):
            piece = slice(n * pillars, (n + 1) * pillars)
            normed = (lifted[:, piece] - centre) * scale + shift
            act = normed * sigmoid(normed)
            acts[:, piece] = act
            top = jnp.maximum(top, jnp.where(limit > n, act, -jnp.inf))
        total = jnp.zeros((channels, pillars), F32)
        for n in range(depth):
            piece = slice(n * pillars, (n + 1) * pillars)
            total = total + jnp.where(limit > n, jnp.exp(acts[:, piece] - top), 0.0)
        result = top + jnp.log(total)
        pooled[micro] = result
        parts = [jnp.zeros((channels, pillars), F32)] * micros
        parts[micro] = result.astype(BF16).astype(F32)
        stacked.append(jnp.transpose(jnp.concatenate(parts, axis=0)))
    values = jnp.concatenate(stacked, axis=0).astype(BF16)
    for group in range(3):
        place = lax.broadcasted_iota(jnp.int32, (rows_out, pillars), 0) + (group - 1) * capacity
        chosen = jnp.concatenate(
            [jnp.where(place.astype(F32) == row, 1.0, 0.0) for row in slot_rows], axis=1
        ).astype(BF16)
        send[:, group * LANES : (group + 1) * LANES] = dot(chosen, values).astype(BF16)


def own_stats(ref, first_row, rows, send):
    micros, _, channels, width = ref.shape
    sums, squares = [], []
    for micro in range(micros):
        total = fold(ref[micro, first_row])
        for row in range(first_row + 1, first_row + rows):
            total = total + fold(ref[micro, row])
        sums.append(total * (1.0 / (rows * width)))
    means = [jnp.sum(total, axis=1, keepdims=True) for total in sums]
    for micro in range(micros):
        spread = jnp.zeros(sums[micro].shape, F32)
        for row in range(first_row, first_row + rows):
            away = ref[micro, row] - means[micro]
            spread = spread + fold(away * away)
        squares.append(spread)
    if channels == LANES:
        send_all(send, [row_of(part) for part in sums + squares])
    else:
        send_all(send, [row_of(*sums), row_of(*squares)])


def expand(taps, weight):
    channels, length = taps.shape
    gap = jnp.zeros((channels, length // 3), BF16)
    weight[0:channels] = jnp.concatenate([taps[...], gap], axis=1)
    weight[channels : 2 * channels] = jnp.concatenate([gap, taps[...]], axis=1)


def conv_pair(source, weight, micro, at, channels):
    window = source[micro, at : at + 4].reshape(12 * channels, source.shape[3])
    return dot(weight[...], window)


def conv_rows(source, weight, out, shape):
    micros, high, channels, width = shape
    for micro in range(micros):
        for at in range(0, high, 2):
            both = conv_pair(source, weight, micro, at, channels)
            out[micro, at] = both[:channels].astype(out.dtype)
            out[micro, at + 1] = both[channels:].astype(out.dtype)


def canvas_kernel(found, where_rows, l_first_in, out, kept, send, canvas, l_first, *, rows):
    expand(l_first_in, l_first)
    columns = jnp.transpose(where_rows[...])
    scenes, high, channels, width = out.shape
    masks = edges(channels, width)
    slots = found.shape[0]
    lane = lax.broadcasted_iota(jnp.int32, (slots, width), 1).astype(F32)
    for group in range(3):
        values = jnp.transpose(found[:, group * LANES : (group + 1) * LANES].astype(F32))
        first, count = ((rows - 2, 2), (0, rows), (0, 2))[group]
        for scene in range(scenes):
            at = 2 * group + scene
            column = columns[:, at : at + 1] - 1.0
            column = column - jnp.floor(column * (1.0 / width)) * width
            row = jnp.floor((where_rows[at : at + 1] - 1.0) * (1.0 / width))
            mine = values[scene * channels : (scene + 1) * channels]
            placed = jnp.concatenate(
                [jnp.where(row == r * 1.0, mine, 0.0) for r in range(first, first + count)], axis=0
            ).astype(BF16)
            chosen = jnp.where(lane == column, 1.0, 0.0).astype(BF16)
            grid = dot(placed, chosen).astype(BF16)
            start = (0, 2, rows + 2)[group]
            for r in range(count):
                row = grid[r * channels : (r + 1) * channels]
                canvas[scene, start + r] = spread(row, masks)
                kept[scene, start + r] = row
    conv_rows(canvas, l_first, out, out.shape)
    own_stats(out, 1, rows, send)


def second_kernel(found, cols, first_out, l_second_in, out, kept, slopes, stats, send, acts, l_second,
                  *, rows, tiles):
    expand(l_second_in, l_second)
    micros, high, channels, width = first_out.shape
    tile = lax.axis_index("tile")
    turned = stat_columns(found, float(rows * width))
    stats[...] = turned
    masks = edges(channels, width)
    for micro in range(micros):
        part = slice(micro * channels, (micro + 1) * channels)
        centre = turned[part, 0:1]
        scale = turned[part, 1:2] * cols[0:channels, 2:3]
        shift = cols[0:channels, 3:4]

        for row in range(high):
            normed = (first_out[micro, row] - centre) * scale + shift
            gate = sigmoid(normed)
            act = normed * gate
            slopes[micro, row] = gate + act * (1.0 - gate)
            if row == 0 or row == high - 1:
                act = act * inside(tile, row - 1, (tiles, rows))
            act = act.astype(BF16)
            acts[micro, row] = spread(act, masks)
            kept[micro, row] = act
    conv_rows(acts, l_second, out, out.shape)
    own_stats(out, 0, rows, send)


def up_kernel(found, cols, second_out, w_up, acts, upper, slopes, plain, crossed, stats, send, *, rows):
    micros, _, channels, width = second_out.shape
    peers = send.shape[0]
    each = crossed.shape[0] // peers
    turned = stat_columns(found, float(rows * width))
    stats[...] = turned
    gain, shift = cols[0:channels, 4:5], cols[0:channels, 5:6]
    lines = []
    for micro in range(micros):
        part = slice(micro * channels, (micro + 1) * channels)
        centre, rstd = turned[part, 0:1], turned[part, 1:2]
        slope_sum = jnp.zeros((channels, LANES), F32)
        unit_sum = jnp.zeros((channels, LANES), F32)
        for row in range(rows):
            unit = (second_out[micro, row] - centre) * rstd
            normed = unit * gain + shift
            gate = sigmoid(normed)
            act = normed * gate
            slope = gate + act * (1.0 - gate)
            sloped = slope * unit
            slope_sum = slope_sum + fold(slope)
            unit_sum = unit_sum + fold(sloped)
            slopes[micro, row] = jnp.concatenate([slope, sloped], axis=0)
            act = act.astype(BF16)
            acts[micro, row] = act
            upper[micro, row] = dot(w_up[...], act)
        lines.append(row_of(slope_sum, unit_sum).astype(BF16).astype(F32))
        crossed[micro * channels : (micro + 1) * channels] = dot_lanes(
            jnp.concatenate([acts[micro, row] for row in range(rows)], axis=1),
            jnp.concatenate([slopes[micro, row].astype(BF16) for row in range(rows)], axis=1),
        )
    plain[...] = jnp.concatenate(lines, axis=0)
    used = micros * channels
    if crossed.shape[0] > used:
        crossed[used:] = jnp.zeros((crossed.shape[0] - used, LANES), F32)
    if 2 * micros + each < send.shape[1]:
        send[...] = jnp.zeros(send.shape, F32)
    for peer in range(peers):
        send[peer, 2 * micros : 2 * micros + each] = crossed[peer * each : (peer + 1) * each]
    own_stats(upper, 0, rows, send)


def exact_rows(rows):
    high = rows.astype(BF16).astype(F32)
    return [high, rows - high]


def top_kernel(
    found, cols, upper, cot, slopes, plain, w_up_t, features, grads, mixed, stats, send, ordered, *, rows, each
):
    micros, _, wide, width = upper.shape
    channels = w_up_t.shape[0]
    lines = []
    for micro in range(micros):
        lines += list(pooled_stats(found[:, micro, :], found[:, micros + micro, :], float(rows * width)))
    turned = columns_of(lines)
    stats[...] = turned
    gain, shift = cols[:, 6:7], cols[:, 7:8]
    gain_rows, shift_rows, mixed_rows = [], [], []
    for micro in range(micros):
        centre, rstd = turned[:, 2 * micro : 2 * micro + 1], turned[:, 2 * micro + 1 : 2 * micro + 2]
        factor = gain * rstd
        gain_sum = jnp.zeros((wide, LANES), F32)
        shift_sum = jnp.zeros((wide, LANES), F32)
        mixed_sum = jnp.zeros((2 * channels, LANES), F32)
        for row in range(rows):
            unit = (upper[micro, row] - centre) * rstd
            normed = unit * gain + shift
            gate = sigmoid(normed)
            act = normed * gate
            grad = cot[micro, row].astype(F32) * (gate + act * (1.0 - gate))
            for j in range(width // LANES):
                ordered[micro, j, pl.ds(row, wide, stride=rows), :] = act[:, j * LANES : (j + 1) * LANES]
            grads[micro, row] = grad
            gain_sum = gain_sum + fold(grad * unit)
            shift_sum = shift_sum + fold(grad)
            below = dot(w_up_t[...], (grad * factor).astype(BF16))
            mixed_sum = mixed_sum + fold(
                slopes[micro, row] * jnp.concatenate([below, below], axis=0)
            )
        gain_rows.append(row_of(gain_sum))
        shift_rows.append(row_of(shift_sum))
        mixed_rows.append(row_of(mixed_sum).astype(BF16).astype(F32))
        line = jnp.concatenate([ordered[micro, j].astype(BF16) for j in range(width // LANES)], axis=1)
        features[micro, 0] = line.reshape(wide, rows, width)
    mixed[...] = jnp.concatenate(mixed_rows, axis=0)
    rows_out = jnp.concatenate(gain_rows + shift_rows, axis=0)
    crossed = jnp.sum(found[:, 2 * micros : 2 * micros + each, :], axis=0)
    rest = send.shape[1] - 6 * micros - each
    block = exact_rows(rows_out) + mixed_rows + [plain[...], crossed]
    if rest > 0:
        block.append(jnp.zeros((rest, LANES), F32))
    block = jnp.concatenate(block, axis=0)
    send[...] = jnp.broadcast_to(block.astype(BF16)[None], send.shape)


def low_rows(turned, value_of, values, stats, gain, low, high, first, rows, tiles):
    micros, _, channels, width = values.shape
    tile = lax.axis_index("tile")
    masks = edges(channels, width)
    for micro in range(micros):
        part = slice(micro * channels, (micro + 1) * channels)
        centre, rstd = stats[part, 0:1], stats[part, 1:2]
        factor = gain * rstd
        slope_part, shift_part = rstd * turned[part, 0:1], turned[part, 1:2]
        for index in range(high):
            grad, value = value_of(micro, index)
            grad = factor * (grad - shift_part - (value - centre) * slope_part)
            if index + first < 0 or index + first >= rows:
                grad = grad * inside(tile, index + first, (tiles, rows))
            low[micro, index] = spread(grad.astype(BF16), masks)


def first_units(first_out, stats, micro, channels):
    part = slice(micro * channels, (micro + 1) * channels)
    centre, rstd = stats[part, 0:1], stats[part, 1:2]
    return lambda row: (first_out[micro, row] - centre) * rstd


def second_sums(total, weight, factors, stats, micro, micros, count):
    channels = weight.shape[1]
    factor, centre = factors[micro], stats[:, 2 * micro : 2 * micro + 1]
    columns = jnp.transpose(jnp.concatenate([total, jnp.zeros((8 - total.shape[0], LANES), F32)], axis=0))
    beta = factor * stats[:, 2 * micro + 1 : 2 * micro + 2] * columns[:, micro : micro + 1] * (1.0 / count)
    alpha = factor * columns[:, micros + micro : micros + micro + 1] * (1.0 / count)
    square = lax.dot_general(
        weight * beta, weight, (((0,), (0,)), ((), ())),
        preferred_element_type=F32, precision=lax.Precision.HIGHEST,
    )
    square = jnp.concatenate([square, square], axis=1)
    line = jnp.sum(weight * (alpha - beta * centre), axis=0, keepdims=True)
    line = jnp.concatenate([line, line], axis=1)

    def give(mixed, plain, crossed):
        mine = crossed[micro * channels : (micro + 1) * channels]
        return mixed - plain * line - jnp.sum(square * mine, axis=0, keepdims=True)

    return give


def middle_back_kernel(
    found, cols, grads, upper, top_stats, second_out, second_stats, slopes, w_up, w_up_t,
    own_mixed, own_plain, own_crossed, second_act, acts, first_out, first_stats, first_slopes, b_second_in,
    out, top_grad, weight_grad, top_gain_grad, top_shift_grad, expected, send,
    low, top_low, extras, second_dz, b_second, *, rows, tiles, each
):
    expand(b_second_in, b_second)
    scene = lax.axis_index("scene")
    micros, _, wide, width = grads.shape
    channels = second_out.shape[2]
    peers = found.shape[0]
    count = float(peers * rows * width)
    kept = 2 * micros
    total = jnp.sum(found[...].astype(F32), axis=0)
    mixed, plain = total[2 * kept : 2 * kept + micros], total[2 * kept + micros : 3 * kept]
    total = total[0:kept] + total[kept : 2 * kept]
    crossed = jnp.concatenate(
        [
            found[peer].astype(F32)[3 * kept : 3 * kept + each]
            for peer in range(-(-micros * channels // each))
        ],
        axis=0,
    )
    own_half(total[0:1] + total[1:2], scene, top_gain_grad)
    own_half(total[2:3] + total[3:4], scene, top_shift_grad)
    factors = [cols[:, 6:7] * top_stats[:, 2 * micro + 1 : 2 * micro + 2] for micro in range(micros)]
    wide_weight = w_up[...].astype(F32)
    turned = columns_of([total[index : index + 1] for index in range(2 * micros)]) * (1.0 / count)
    gain = cols[0:channels, 4:5]
    masks = edges(channels, width)
    second_rows = []
    for micro in range(micros):
        top_centre = top_stats[:, 2 * micro : 2 * micro + 1]
        top_slope = top_stats[:, 2 * micro + 1 : 2 * micro + 2] * turned[:, micro : micro + 1]
        top_shift = turned[:, micros + micro : micros + micro + 1]
        part = slice(micro * channels, (micro + 1) * channels)
        centre, rstd = second_stats[part, 0:1], second_stats[part, 1:2]
        gain_sum = jnp.zeros((channels, LANES), F32)
        shift_sum = jnp.zeros((channels, LANES), F32)
        for row in range(rows):
            grad = factors[micro] * (
                grads[micro, row] - top_shift - (upper[micro, row] - top_centre) * top_slope
            )
            grad = grad.astype(BF16)
            top_low[micro, row] = grad
            unit = (second_out[micro, row] - centre) * rstd
            grad = dot(w_up_t[...], grad) * slopes[micro, row, 0:channels]
            second_dz[micro, row] = grad
            shift_sum = shift_sum + fold(grad)
            gain_sum = gain_sum + fold(grad * unit)
        second_rows.append((shift_sum, gain_sum))
    parts = []
    for micro in range(micros):
        give = second_sums(total, wide_weight, factors, top_stats, micro, micros, count)
        whole = give(mixed[micro : micro + 1], plain[micro : micro + 1], crossed)
        extra = row_of(*second_rows[micro]) - give(
            own_mixed[micro : micro + 1], own_plain[micro : micro + 1], own_crossed[...]
        )
        expected[micro : micro + 1] = whole
        extras[micro : micro + 1] = extra
        parts.append(whole * (1.0 / count) + extra * (1.0 / (rows * width)))
    parts = columns_of(parts)
    for micro in range(micros):
        part = slice(micro * channels, (micro + 1) * channels)
        centre, rstd = second_stats[part, 0:1], second_stats[part, 1:2]
        factor = gain * rstd
        shift_part = parts[0:channels, micro : micro + 1]
        slope_part = parts[channels : 2 * channels, micro : micro + 1] * rstd
        for row in range(rows):
            grad = factor * (
                second_dz[micro, row] - shift_part - (second_out[micro, row] - centre) * slope_part
            )
            low[micro, row] = spread(grad.astype(BF16), masks)
    first_back(
        low, top_low, second_act, acts, first_out, first_stats, first_slopes, b_second, extras,
        out, top_grad, weight_grad, send, rows, tiles,
    )


def first_back(
    low, top_low, second_act, acts, first_out, first_stats, slopes, b_second, extras,
    out, top_grad, weight_grad, send, rows, tiles
):
    tile = lax.axis_index("tile")
    micros, _, channels, width = first_out.shape
    half = 6 * channels
    gain_sums, shift_sums = [], []
    for micro in range(micros):
        units = first_units(first_out, first_stats, micro, channels)
        gain_sum = jnp.zeros((channels, LANES), F32)
        shift_sum = jnp.zeros((channels, LANES), F32)
        for at in range(0, rows + 2, 2):
            if at == 0:
                parts = dot(b_second[:, half:], low[micro, 0:2].reshape(half, width))
            elif at == rows:
                parts = dot(b_second[:, :half], low[micro, rows - 2 : rows].reshape(half, width))
            else:
                parts = conv_pair(low, b_second, micro, at - 2, channels)
            for j in range(2):
                grad = parts[channels * j : channels * (j + 1)] * slopes[micro, at + j]
                if at + j == 0 or at + j == rows + 1:
                    grad = grad * inside(tile, at + j - 1, (tiles, rows))
                out[micro, at + j] = grad
                gain_sum = gain_sum + fold(grad * units(at + j))
                shift_sum = shift_sum + fold(grad)
        gain_sums.append(gain_sum)
        shift_sums.append(shift_sum)
        product = dot_lanes(
            jnp.concatenate([top_low[micro, row] for row in range(rows)], axis=1),
            jnp.concatenate([second_act[micro, row] for row in range(rows)], axis=1),
        )
        top_grad[...] = product if micro == 0 else top_grad[...] + product
    conv_grad(low, 0, acts, 0, weight_grad, rows)
    send_all(send, [row_of(*gain_sums), row_of(*shift_sums)] + [extras[m : m + 1] for m in range(micros)])


def conv_grad(low, low_first, values, value_first, total, rows):
    micros, _, channels, width = values.shape
    for micro in range(micros):
        grads = jnp.concatenate([low[micro, row + low_first] for row in range(rows)], axis=1)
        windows = jnp.concatenate(
            [
                values[micro, row + value_first : row + value_first + 3].reshape(3 * channels, width)
                for row in range(rows)
            ],
            axis=1,
        )
        product = dot_lanes(grads, windows)
        total[...] = product if micro == 0 else total[...] + product


def half_rows(total, half, scene):
    channels = 2 * half
    start = scene * half
    mine = jnp.concatenate(
        [total[b * channels + start : b * channels + start + half, :] for b in range(2, -1, -1)], axis=0
    )
    wing = mine[:, LANES:]
    cut = wing.shape[0] // 2
    return [mine[:, :LANES], jnp.concatenate([wing[:cut], wing[cut:]], axis=1)]


def pick_kernel(
    found, cols, grads, first_out, first_stats, b_first_in, where_rows,
    canvas, second_grad, top_grad, expected,
    send, gain_grad, shift_grad, second_gain_grad, second_shift_grad, low, grid, b_first, first_grad, whole,
    *, rows, tiles, each
):
    expand(b_first_in, b_first)
    scene = lax.axis_index("scene")
    micros, high, channels, width = grads.shape
    sums = sum_rows(found, 2 + micros)
    second = sum(sums[2:]) + jnp.sum(expected[...], axis=0, keepdims=True)
    own_half(second[:, :channels], scene, second_shift_grad)
    own_half(second[:, channels:], scene, second_gain_grad)
    sums = sums[:2]
    own_half(sums[0][:, :channels] + sums[0][:, channels:], scene, gain_grad)
    own_half(sums[1][:, :channels] + sums[1][:, channels:], scene, shift_grad)
    turned = columns_of(sums) * (1.0 / (found.shape[0] * rows * width))
    masks = edges(channels, width)
    for micro in range(micros):
        part = slice(micro * channels, (micro + 1) * channels)
        centre, rstd = first_stats[part, 0:1], first_stats[part, 1:2]
        factor = cols[0:channels, 2:3] * rstd
        slope_part, shift_part = rstd * turned[part, 0:1], turned[part, 1:2]
        for row in range(high):
            grad = grads[micro, row]
            if 1 <= row <= rows:
                grad = grad - shift_part - (first_out[micro, row] - centre) * slope_part
            low[micro, row] = spread((factor * grad).astype(BF16), masks)
    half = 6 * channels
    for micro in range(micros):
        for at in range(0, rows + 4, 2):
            if at == 0:
                parts = dot(b_first[:, half:], low[micro, 0:2].reshape(half, width))
            elif at == rows + 2:
                parts = dot(b_first[:, :half], low[micro, rows : rows + 2].reshape(half, width))
            else:
                parts = conv_pair(low, b_first, micro, at - 2, channels)
            grid[micro, at] = parts[:channels].astype(BF16)
            grid[micro, at + 1] = parts[channels:].astype(BF16)
    conv_grad(low, 0, canvas, 0, first_grad, high)
    half = channels // 2
    for s in range(2):
        parts = half_rows(first_grad, half, s) + half_rows(second_grad, half, s)
        mine = top_grad[s * channels : (s + 1) * channels, :]
        parts.append(jnp.concatenate([mine[:half], mine[half:]], axis=1))
        parts = jnp.concatenate(parts, axis=0)
        whole[s, 0 : parts.shape[0]] = parts
        if whole.shape[1] > parts.shape[0]:
            whole[s, parts.shape[0] :] = jnp.zeros((whole.shape[1] - parts.shape[0], LANES), F32)
    columns = jnp.transpose(where_rows[...])
    slots = columns.shape[0]
    lane = lax.broadcasted_iota(jnp.int32, (slots, width), 1).astype(F32)
    groups = []
    for group in range(3):
        start, first, count = ((0, rows - 2, 2), (2, 0, rows), (rows + 2, 0, 2))[group]
        picked = []
        for micro in range(micros):
            at = 2 * group + micro
            column = columns[:, at : at + 1] - 1.0
            column = column - jnp.floor(column * (1.0 / width)) * width
            chosen = jnp.where(lane == column, 1.0, 0.0).astype(BF16)
            place = jnp.floor((where_rows[at : at + 1] - 1.0) * (1.0 / width))
            here = dot_lanes(grid[micro, start : start + count].reshape(count * channels, width), chosen)
            total = jnp.zeros((channels, slots), F32)
            for r in range(count):
                total = total + jnp.where(
                    place == (first + r) * 1.0, here[r * channels : (r + 1) * channels], 0.0
                )
            picked.append(total)
        groups.append(jnp.transpose(jnp.concatenate(picked, axis=0)))
    capacity = slots // tiles
    block = send.shape[1]

    def filled(parts):
        missing = block - sum(part.shape[0] for part in parts)
        if missing > 0:
            parts = parts + [jnp.zeros((missing, LANES), F32)]
        return jnp.concatenate(parts, axis=0).astype(BF16)

    for spot in range(tiles):
        mine = slice(spot * capacity, (spot + 1) * capacity)
        send[2 * spot + scene] = filled([picked[mine] for picked in groups])
        send[2 * spot + 1 - scene] = filled([whole[s, spot * each : (spot + 1) * each] for s in range(2)])


def pillar_weights_kernel(rows, w_pillar, cols, pooled, out, lifted):
    micros, channels, wide = out.shape
    pillars = pooled.shape[2]
    inputs = w_pillar.shape[1]
    gain, shift = cols[0:channels, 0:1], cols[0:channels, 1:2]
    for micro in range(micros):
        lifted[...] = dot(w_pillar[...], rows[micro, 0:inputs])
        _, limit = pillar_notes(rows, micro, inputs, pillars)
        centre, rstd = pooled[micros + micro, :, 0:1], pooled[micros + micro, :, 1:2]
        pool = pooled[micro]
        for n in range(wide // pillars):
            piece = slice(n * pillars, (n + 1) * pillars)
            normed = (lifted[:, piece] - centre) * rstd * gain + shift
            gate = sigmoid(normed)
            act = normed * gate
            slope = gate + act * (1.0 - gate)
            out[micro, :, piece] = jnp.where(limit > n, jnp.exp(act - pool) * slope, 0.0).astype(BF16)


def pillar_back_kernel(found, rows, w_pillar, cols, pooled, factors, send, grads, lifted, *, capacity, each):
    micros = rows.shape[0]
    _, channels, pillars = pooled.shape
    stats = pooled.at[micros : 2 * micros]
    inputs = w_pillar.shape[1]
    depth = rows.shape[2] // pillars
    scene = lax.axis_index("scene")
    peers = found.shape[0]
    slot_count = peers // 2 * capacity
    blocks = [found[2 * t + scene].astype(F32) for t in range(peers // 2)]
    before, own, after = [
        jnp.concatenate([block[group * capacity : (group + 1) * capacity] for block in blocks], axis=0)
        for group in range(3)
    ]
    gap = jnp.zeros((capacity, LANES), F32)
    returned = (
        own
        + jnp.concatenate([before[capacity:], gap], axis=0)
        + jnp.concatenate([gap, after[: slot_count - capacity]], axis=0)
    )
    turned = jnp.transpose(returned)
    place = lax.broadcasted_iota(jnp.int32, (slot_count, pillars), 0).astype(F32)
    gain = cols[0:channels, 0:1]
    gain_sums, shift_sums = [], []
    outer = jnp.zeros((16, channels), F32)
    for micro in range(micros):
        lifted[...] = dot(w_pillar[...], rows[micro, 0:inputs])
        slot, _ = pillar_notes(rows, micro, inputs, pillars)
        chosen = jnp.where(place == slot, 1.0, 0.0).astype(BF16)
        back = dot(turned[micro * channels : (micro + 1) * channels].astype(BF16), chosen)
        centre, rstd = stats[micro, :, 0:1], stats[micro, :, 1:2]
        gain_sum = jnp.zeros((channels, pillars), F32)
        shift_sum = jnp.zeros((channels, pillars), F32)
        for n in range(depth):
            piece = slice(n * pillars, (n + 1) * pillars)
            grad = back * factors[micro, :, piece].astype(F32)
            grads[micro, :, piece] = grad
            gain_sum = gain_sum + grad * (lifted[:, piece] - centre)
            shift_sum = shift_sum + grad
        gain_sum = gain_sum * rstd
        gain_sums.append(gain_sum)
        shift_sums.append(shift_sum)
        scale = jnp.transpose(jnp.broadcast_to(rstd * gain, (channels, LANES)))[0:1]
        outer = outer + dot_lanes(rows[micro], grads[micro].astype(BF16)) * scale
    exact = jnp.concatenate([row_of(*gain_sums), row_of(*shift_sums)], axis=0)
    lines = [jnp.concatenate([outer[k : k + 1], outer[k + 1 : k + 2]], axis=1) for k in range(0, 10, 2)]
    weights = found[1 - scene].astype(F32)
    for t in range(1, peers // 2):
        weights = weights + found[2 * t + 1 - scene].astype(F32)
    rest = send.shape[2] - 9 - each
    for s in range(2):
        block = exact_rows(exact) + lines + [weights[s * each : (s + 1) * each]]
        if rest > 0:
            block.append(jnp.zeros((rest, LANES), F32))
        block = jnp.concatenate(block, axis=0).astype(BF16)
        send[:, s] = jnp.broadcast_to(block[None], (send.shape[0],) + block.shape)


def points_kernel(
    found, rows, grads, w_pillar, cols, pooled,
    points_grad, pillar_grad, gain_grad, shift_grad, first_grad, second_grad, up_grad, lifted, *, each
):
    scene = lax.axis_index("scene")
    micros, channels, _ = grads.shape
    stats = pooled.at[micros : 2 * micros]
    _, _, inputs, depth, pillars = points_grad.shape
    half = channels // 2
    total = jnp.sum(found[...].astype(F32), axis=0)
    total = jnp.concatenate([total[0:2] + total[2:4], total[4:9]], axis=0)
    own_half(total[0:1, :channels] + total[0:1, channels:], scene, gain_grad)
    own_half(total[1:2, :channels] + total[1:2, channels:], scene, shift_grad)
    turned = jnp.transpose(jnp.concatenate([total, jnp.zeros((1, LANES), F32)], axis=0))
    weight_grad = jnp.concatenate(
        [turned[(k % 2) * channels : (k % 2 + 1) * channels, 2 + k // 2 : 3 + k // 2] for k in range(inputs)],
        axis=1,
    )
    weight = jnp.transpose(w_pillar[...].astype(F32)).astype(BF16)
    for micro in range(micros):
        lifted[...] = dot(w_pillar[...], rows[micro, 0:inputs])
        part = slice(micro * channels, (micro + 1) * channels)
        centre, rstd, inverse = stats[micro, :, 0:1], stats[micro, :, 1:2], stats[micro, :, 2:3]
        factor = cols[0:channels, 0:1] * rstd
        gain_part, shift_part = turned[part, 0:1], turned[part, 1:2]
        spun, mean = stats[micro, :, 16 : 16 + inputs], stats[micro, :, 32 : 32 + inputs]
        weight_grad = weight_grad - factor * (shift_part * mean + gain_part * rstd * spun)
        gain_part, shift_part = gain_part * inverse * rstd, shift_part * inverse
        _, limit = pillar_notes(rows, micro, inputs, pillars)
        for n in range(depth):
            piece = slice(n * pillars, (n + 1) * pillars)
            low = factor * (grads[micro, :, piece] - shift_part - (lifted[:, piece] - centre) * gain_part)
            low = jnp.where(limit > n, low, 0.0).astype(BF16)
            points_grad[micro, 0, :, n, :] = dot(weight, low)
    weight_grad = jnp.concatenate([weight_grad, jnp.zeros((channels, LANES - inputs), F32)], axis=1)
    weight_grad = jnp.transpose(weight_grad)[0:inputs]
    pillar_grad[...] = jnp.where(scene == 0, weight_grad[:, :half], weight_grad[:, half:])
    whole = jnp.concatenate(
        [
            (found[2 * t].astype(F32) + found[2 * t + 1].astype(F32))[9 : 9 + each]
            for t in range(found.shape[0] // 2)
        ],
        axis=0,
    )
    for index, out in enumerate((first_grad, second_grad)):
        base = index * 9 * half * channels // LANES
        lead = 3 * half
        mine = whole[base : base + lead]
        wing = whole[base + lead : base + lead + lead // 2]
        wing = jnp.concatenate([wing[:, :channels], wing[:, channels:]], axis=0)
        both = jnp.concatenate([mine, wing], axis=1)
        for a in range(3):
            for b in range(3):
                at = (3 * a + b) * channels
                out[:, at : at + channels] = both[b * half : (b + 1) * half, a * channels : (a + 1) * channels]
    base = 2 * 9 * half * channels // LANES
    top = whole[base : base + half]
    up_grad[...] = jnp.concatenate([top[:, :channels], top[:, channels:]], axis=0)


def swap(blocks, axes):
    return lax.all_to_all(blocks, axes, split_axis=0, concat_axis=0)


def shards(
    points, point_counts, pillar_tile, pillar_cell,
    pillar_weight, pillar_gain, pillar_shift,
    first_weight, first_gain, first_shift,
    second_weight, second_gain, second_shift,
    up_weight, up_gain, up_shift, cotangent,
):
    micros, _, inputs, depth, pillars = points.shape
    channels = up_weight.shape[1]
    upper = cotangent.shape[2]
    rows, width = cotangent.shape[3:]
    tiles = lax.axis_size("tile")
    scenes = lax.axis_size("scene")
    peers = tiles * scenes
    capacity = 2 * pillars // tiles
    slot_count = tiles * capacity
    half = channels // 2

    def vmem(shape, dtype):
        return pltpu.VMEM(shape, dtype)

    def grid(high, dtype=F32, lead=channels):
        return ((micros, high, lead, width), dtype)

    sums = ((peers, 2, LANES), F32)
    sources = (pillar_tile, pillar_cell, point_counts, points)
    wide = vmem((inputs * depth, pillars), F32)
    (moments,) = run(
        functools.partial(moments_kernel, capacity=capacity),
        [((tiles, scenes, 4, LANES), F32)],
        *sources,
        hbm=range(len(sources)), copies=len(sources), limit=WIDE_LIMIT,
        scratch=[vmem(source.shape, source.dtype) for source in sources] + [wide],
    )
    sources = (
        pillar_tile, point_counts, points,
        first_weight, second_weight, up_weight, pillar_weight.T,
        pillar_gain, pillar_shift, first_gain, first_shift, second_gain, second_shift, up_gain, up_shift,
    )
    packed, point_rows = run(
        functools.partial(pack_kernel, capacity=capacity),
        [((layout(half, channels)[-1] + 16, LANES), BF16), ((micros, 16, depth * pillars), BF16)],
        *sources,
        hbm=range(len(sources)), copies=len(sources), limit=WIDE_LIMIT,
        scratch=[vmem(source.shape, source.dtype) for source in sources] + [wide],
        cost=pl.CostEstimate(flops=10**7, bytes_accessed=10**6, transcendentals=0),
    )
    moments = swap(moments.reshape(peers, 4, LANES), BOTH)
    both = lax.all_gather(packed, "scene")
    taps = ((2 * channels, 12 * channels), BF16)
    compact = ((channels, 9 * channels), BF16)
    w_pillar, cols, l_first, l_second, b_first, b_second, w_up, w_up_t = run(
        functools.partial(unpack_kernel, inputs=inputs),
        [
            ((channels, inputs), BF16), ((LANES, 8), F32), compact, compact, compact, compact,
            ((upper, channels), BF16), ((channels, upper), BF16),
        ],
        both,
    )
    cot = cotangent[:, 0].transpose(0, 2, 1, 3)

    send, pooled = run(
        functools.partial(pillar_kernel, capacity=capacity),
        [((slot_count, 3 * LANES), BF16), ((2 * micros, channels, pillars), F32)],
        moments, point_rows, w_pillar, cols,
        scratch=[vmem((channels, depth * pillars), F32), vmem((channels, depth * pillars), F32)],
    )
    arrived = swap(send.reshape(tiles, capacity, 3 * LANES), "tile").reshape(slot_count, 3 * LANES)
    (cell_rows,) = run(
        functools.partial(cells_kernel, capacity=capacity),
        [((8, slot_count), F32)],
        moments,
        cost=pl.CostEstimate(flops=10**7, bytes_accessed=10**6, transcendentals=0),
    )
    (factors,) = run(
        pillar_weights_kernel,
        [((micros, channels, depth * pillars), BF16)],
        point_rows, w_pillar, cols, pooled,
        scratch=[vmem((channels, depth * pillars), F32)],
        cost=pl.CostEstimate(flops=10**7, bytes_accessed=10**6, transcendentals=0),
    )
    arrived, cot, factors = lax.optimization_barrier((arrived, cot, factors))

    first_out, canvas, send = run(
        functools.partial(canvas_kernel, rows=rows),
        [grid(rows + 2), grid(rows + 4, BF16), sums],
        arrived, cell_rows, l_first,
        scratch=[vmem(*grid(rows + 4, BF16, 3 * channels)), vmem(*taps)],
    )
    second_out, first_act, first_slopes, first_stats, send = run(
        functools.partial(second_kernel, rows=rows, tiles=tiles),
        [grid(rows), grid(rows + 2, BF16), grid(rows + 2), ((LANES, 8), F32), sums],
        swap(send, BOTH), cols, first_out, l_second,
        scratch=[vmem(*grid(rows + 2, BF16, 3 * channels)), vmem(*taps)],
    )
    part = -(-micros * channels // peers)
    second_act, up_out, slopes, plain, crossed, second_stats, send = run(
        functools.partial(up_kernel, rows=rows),
        [
            grid(rows, BF16), grid(rows, F32, upper), grid(rows, F32, 2 * channels), ((micros, LANES), F32),
            ((peers * part, LANES), F32), ((LANES, 8), F32), ((peers, -(-(2 * micros + part) // 8) * 8, LANES), F32),
        ],
        swap(send, BOTH), cols, second_out, w_up,
    )
    features, grads, mixed, top_stats, send = run(
        functools.partial(top_kernel, rows=rows, each=part),
        [
            ((micros, 1, upper, rows, width), BF16), grid(rows, F32, upper), ((micros, LANES), F32),
            ((LANES, 8), F32),
            ((peers, -(-(6 * micros + part) // 8) * 8, LANES), BF16),
        ],
        swap(send, BOTH), cols, up_out, cot, slopes, plain, w_up_t,
        scratch=[vmem((micros, width // LANES, upper * rows, LANES), F32)],
    )
    vector, top_vector, matrix = ((half,), F32), ((upper // 2,), F32), ((half, 9 * channels), F32)
    cross = ((3 * channels, 3 * channels), F32)
    first_dz, top_grad, second_cross, up_gain_grad, up_shift_grad, expected, send = run(
        functools.partial(middle_back_kernel, rows=rows, tiles=tiles, each=part),
        [
            grid(rows + 2), ((upper, channels), F32), cross, top_vector, top_vector, ((micros, LANES), F32),
            ((peers, 2 + micros, LANES), F32),
        ],
        swap(send, BOTH), cols, grads, up_out, top_stats, second_out, second_stats, slopes, w_up, w_up_t,
        mixed, plain, crossed, second_act, first_act, first_out, first_stats, first_slopes, b_second,
        scratch=[
            vmem(*grid(rows, BF16, 3 * channels)), vmem(*grid(rows, BF16, upper)), vmem((micros, LANES), F32),
            vmem(*grid(rows)), vmem(*taps),
        ],
    )
    length = (2 * 9 * half * channels + upper * half) // LANES
    each = -(-length // tiles)
    block = -(-max(3 * capacity, 2 * each) // 8) * 8
    send, first_gain_grad, first_shift_grad, second_gain_grad, second_shift_grad = run(
        functools.partial(pick_kernel, rows=rows, tiles=tiles, each=each),
        [((peers, block, LANES), BF16), vector, vector, vector, vector],
        swap(send, BOTH), cols, first_dz, first_out, first_stats, b_first, cell_rows,
        canvas, second_cross, top_grad, expected,
        scratch=[
            vmem(*grid(rows + 2, BF16, 3 * channels)), vmem(*grid(rows + 4, BF16)), vmem(*taps), vmem(*cross),
            vmem((scenes, tiles * each, LANES), F32),
        ],
    )
    block = -(-(9 + each) // 8) * 8
    send, pillar_dz = run(
        functools.partial(pillar_back_kernel, capacity=capacity, each=each),
        [((tiles, scenes, block, LANES), BF16), ((micros, channels, depth * pillars), F32)],
        swap(send, BOTH), point_rows, w_pillar, cols, pooled, factors,
        scratch=[vmem((channels, depth * pillars), F32)],
    )
    points_grad, pillar_grad, pillar_gain_grad, pillar_shift_grad, first_grad, second_grad, up_grad = run(
        functools.partial(points_kernel, each=each),
        [
            ((micros, 1, inputs, depth, pillars), F32), ((inputs, half), F32), vector, vector,
            matrix, matrix, ((upper // 2, channels), F32),
        ],
        swap(send.reshape(peers, block, LANES), BOTH), point_rows, pillar_dz, w_pillar, cols, pooled,
        scratch=[vmem((channels, depth * pillars), F32)],
    )
    return (
        features, points_grad,
        pillar_grad.T, pillar_gain_grad, pillar_shift_grad,
        first_grad, first_gain_grad, first_shift_grad,
        second_grad, second_gain_grad, second_shift_grad,
        up_grad, up_gain_grad, up_shift_grad,
    )


def solution(mesh):
    matrix, vector = P("scene", None), P("scene")
    grid = P(None, "scene", None, "tile", None)
    cloud = P(None, "scene", None, None, "tile")
    pillar = P(None, "scene", "tile")
    weights = (matrix, vector, vector) * 4
    return jax.shard_map(
        shards,
        mesh=mesh,
        in_specs=(cloud, pillar, pillar, pillar) + weights + (grid,),
        out_specs=(grid, cloud) + weights,
        check_vma=False,
    )
```

profile of v0, /device:TPU:0, one launch (start us, length us, event | category | flops | bytes accessed | tf_op | source)
XLA Modules:
  0.0 127.7 jit_solution(7414969436930092519)
XLA Ops:
  0.6 2.5 %shard_map.272 = f32[16,2,4,128]{3,2,1,0:T(4,128)} custom-call(s32[2,1,128]{2,1,0:T(1,128)} %refs_0_.3, s32[2,1,128]{2,1,0:T(1,128)} %refs_1_.2, s32[2,1,128]{2,1,0:T(1,128)} %refs_1_.3, bf16[2,1,9,32,128]{4,3,2,1,0:T(8,128)(2,1)} %refs_2_.3), custom_call_target="tpu_custom_call" | custom-call | tf_op jit(solution)/shard_map/pallas_call | solution.py:26
  3.1 7.3 %all-to-all-start = ((f32[32,4,128]{2,1,0:T(4,128)}), f32[32,4,128]{2,1,0:T(4,128)S(1)}, u32[]{:S(2)}, u32[]{:S(2)}) async-start(f32[32,4,128]{2,1,0:T(4,128)} %bitcast.16), calls=%async_computation | async-start | bytes 131072 | tf_op jit(solution)/shard_map/all_to_all | solution.py:1002
  10.5 2.0 %shard_map.273 = (bf16[416,128]{1,0:T(8,128)(2,1)}, bf16[2,16,4096]{2,1,0:T(8,128)(2,1)}) custom-call(s32[2,1,128]{2,1,0:T(1,128)} %refs_0_.3, s32[2,1,128]{2,1,0:T(1,128)} %refs_1_.3, bf16[2,1,9,32,128]{4,3,2,1,0:T(8,128)(2,1)} %refs_2_.3, bf16[32,576]{1,0:T(8,128)(2,1)} %refs_3_.3, bf16[32,576]{1,0:T(8,128)(2,1)} %refs_4_.1, bf16[64,64]{1,0:T(8,128)(2,1)} %refs_5_.1, ...), custom_call_target="tpu_custom_call" | custom-call | flops 10000000 | bytes 1000000 | tf_op jit(solution)/shard_map/pallas_call | solution.py:26
  12.5 0.0 copy-start.1
  12.5 2.3 %all-gather = bf16[832,128]{1,0:T(8,128)(2,1)S(1)} all-gather(bf16[416,128]{1,0:T(8,128)(2,1)} %get-tuple-element.71), channel_id=2, replica_groups=mesh['tile'=16,'scene'=2] {'scene'}, dimensions={0}, use_global_device_ids=true | all-gather | bytes 319488 | tf_op jit(solution)/shard_map/all_gather | solution.py:1053
  14.8 0.4 shard_map.274
  15.2 2.7 %all-to-all-done.found = f32[32,4,128]{2,1,0:T(4,128)S(1)} async-done(((f32[32,4,128]{2,1,0:T(4,128)}), f32[32,4,128]{2,1,0:T(4,128)S(1)}, u32[]{:S(2)}, u32[]{:S(2)}) %all-to-all-start) | async-done | bytes 65568 | tf_op jit(solution)/shard_map/all_to_all | solution.py:1002
  17.9 0.0 copy-start
  17.9 0.9 copy-done
  18.8 2.9 %shard_map.275 = (bf16[256,384]{1,0:T(8,128)(2,1)}, f32[4,64,128]{2,1,0:T(8,128)S(1)}) custom-call(f32[32,4,128]{2,1,0:T(4,128)S(1)} %all-to-all-done.found, bf16[2,16,4096]{2,1,0:T(8,128)(2,1)S(1)} %copy-done, bf16[64,9]{1,0:T(8,128)(2,1)S(1)} %get-tuple-element.72.w_pillar, f32[128,8]{1,0:T(8,128)S(1)} %get-tuple-element.73.cols), custom_call_target="tpu_custom_call" | custom-call | tf_op jit(solution)/shard_map/pallas_call | solution.py:26
  21.7 4.2 %all-to-all-start.1 = ((bf16[16,16,384]{2,1,0:T(8,128)(2,1)}), bf16[16,16,384]{2,1,0:T(8,128)(2,1)S(1)}, u32[]{:S(2)}, u32[]{:S(2)}) async-start(bf16[16,16,384]{2,1,0:T(8,128)(2,1)} %bitcast.3), calls=%async_computation.1 | async-start | bytes 393216 | tf_op jit(solution)/shard_map/all_to_all | solution.py:1002
  25.9 1.4 %copy.33 = bf16[2,1,128,4,512]{4,2,3,0,1:T(8,128)(2,1)S(1)} copy(bf16[2,1,128,4,512]{4,3,2,1,0:T(4,128)(2,1)} %param.33) | data formatting | bytes 2097152 | tf_op args[16]
  27.3 0.0 copy-done.1
  27.3 1.5 %shard_map.276.factors = bf16[2,64,4096]{2,1,0:T(8,128)(2,1)S(1)} custom-call(bf16[2,16,4096]{2,1,0:T(8,128)(2,1)S(1)} %copy-done.1, bf16[64,9]{1,0:T(8,128)(2,1)S(1)} %get-tuple-element.72.w_pillar, f32[128,8]{1,0:T(8,128)S(1)} %get-tuple-element.73.cols, f32[4,64,128]{2,1,0:T(8,128)S(1)} %get-tuple-element.75.pooled), custom_call_target="tpu_custom_call" | custom-call | flops 10000000 | bytes 1000000 | tf_op jit(solution)/shard_map/pallas_call | solution.py:26
  28.8 0.5 shard_map.277.where_rows
  29.4 5.5 %all-to-all-done.1 = bf16[16,16,384]{2,1,0:T(8,128)(2,1)S(1)} async-done(((bf16[16,16,384]{2,1,0:T(8,128)(2,1)}), bf16[16,16,384]{2,1,0:T(8,128)(2,1)S(1)}, u32[]{:S(2)}, u32[]{:S(2)}) %all-to-all-start.1) | async-done | bytes 196640 | tf_op jit(solution)/shard_map/all_to_all | solution.py:1002
  34.8 1.5 %shard_map.278 = (f32[2,6,64,512]{3,2,1,0:T(8,128)S(1)}, bf16[2,8,64,512]{3,2,1,0:T(8,128)(2,1)S(1)}, f32[32,2,128]{2,1,0:T(2,128)S(1)}) custom-call(bf16[256,384]{1,0:T(8,128)(2,1)S(1)} %bitcast.14, f32[8,256]{1,0:T(8,128)S(1)} %shard_map.277.where_rows, bf16[64,576]{1,0:T(8,128)(2,1)S(1)} %get-tuple-element.77.l_first_in), custom_call_target="tpu_custom_call" | custom-call | tf_op jit(solution)/shard_map/pallas_call | solution.py:26
  36.4 9.4 %all_to_all.45.found = f32[32,2,128]{2,1,0:T(2,128)S(1)} all-to-all(f32[32,2,128]{2,1,0:T(2,128)S(1)} %get-tuple-element.78), channel_id=1, replica_groups=mesh['tile'=16,'scene'=2] {'tile','scene'}, dimensions={0} | all-to-all | bytes 65536 | tf_op jit(solution)/shard_map/all_to_all | solution.py:1002
  45.8 1.5 %shard_map.279 = (f32[2,4,64,512]{3,2,1,0:T(8,128)S(1)}, bf16[2,6,64,512]{3,2,1,0:T(8,128)(2,1)S(1)}, f32[2,6,64,512]{3,2,1,0:T(8,128)S(1)}, f32[128,8]{1,0:T(8,128)S(1)}, f32[32,2,128]{2,1,0:T(2,128)S(1)}) custom-call(f32[32,2,128]{2,1,0:T(2,128)S(1)} %all_to_all.45.found, f32[128,8]{1,0:T(8,128)S(1)} %get-tuple-element.73.cols, ...), custom_call_target="tpu_custom_call" | custom-call | tf_op jit(solution)/shard_map/pallas_call | solution.py:26
  47.4 8.9 %all_to_all.46.found = f32[32,2,128]{2,1,0:T(2,128)S(1)} all-to-all(f32[32,2,128]{2,1,0:T(2,128)S(1)} %get-tuple-element.81), channel_id=1, replica_groups=mesh['tile'=16,'scene'=2] {'tile','scene'}, dimensions={0} | all-to-all | bytes 65536 | tf_op jit(solution)/shard_map/all_to_all | solution.py:1002
  56.3 1.6 %shard_map.280 = (bf16[2,4,64,512]{3,2,1,0:T(8,128)(2,1)S(1)}, f32[2,4,128,512]{3,2,1,0:T(8,128)S(1)}, f32[2,4,128,512]{3,2,1,0:T(8,128)S(1)}, f32[2,128]{1,0:T(...) custom-call(f32[32,2,128]{2,1,0:T(2,128)S(1)} %all_to_all.46.found, ...), custom_call_target="tpu_custom_call" | custom-call | tf_op jit(solution)/shard_map/pallas_call | solution.py:26
  57.9 9.9 %all_to_all.47.found = f32[32,8,128]{2,1,0:T(8,128)S(1)} all-to-all(f32[32,8,128]{2,1,0:T(8,128)S(1)} %get-tuple-element.84), channel_id=1, replica_groups=mesh['tile'=16,'scene'=2] {'tile','scene'}, dimensions={0} | all-to-all | bytes 262144 | tf_op jit(solution)/shard_map/all_to_all | solution.py:1002
  67.9 2.8 %shard_map.281 = (bf16[2,1,128,4,512]{4,3,2,1,0:T(4,128)(2,1)}, f32[2,4,128,512]{3,2,1,0:T(8,128)S(1)}, f32[2,128]{1,0:T(2,128)S(1)}, f32[128,8]{1,0:T(8,128)S(1)}, bf16[32,16,128]{2,1,0:T(8,128)(2,1)S(1)}) custom-call(f32[32,8,128]{2,1,0:T(8,128)S(1)} %all_to_all.47.found, f32[128,8]{1,0:T(8,128)S(1)} %get-tuple-element.73.cols, ...), custom_call_target="tpu_custom_call" | custom-call | tf_op jit(solution)/shard_map/pallas_call | solution.py:26
  70.7 9.9 %all_to_all.48.found = bf16[32,16,128]{2,1,0:T(8,128)(2,1)S(1)} all-to-all(bf16[32,16,128]{2,1,0:T(8,128)(2,1)S(1)} %get-tuple-element.91), channel_id=1, replica_groups=mesh['tile'=16,'scene'=2] {'tile','scene'}, dimensions={0} | all-to-all | bytes 262144 | tf_op jit(solution)/shard_map/all_to_all | solution.py:1002
  80.6 3.7 %shard_map.282 = (f32[2,6,64,512]{3,2,1,0:T(8,128)S(1)}, f32[128,64]{1,0:T(8,128)S(1)}, f32[192,192]{1,0:T(8,128)S(1)}, f32[64]{0:T(128)}, f32[64]{0:T(128)}, /*...) custom-call(bf16[32,16,128]{2,1,0:T(8,128)(2,1)S(1)} %all_to_all.48.found, f32[128,8]{1,0:T(8,128)S(1)} %get-tuple-element.73.cols, ...), custom_call_target="tpu_custom_call" | custom-call | tf_op jit(solution)/shard_map/pallas_call | solution.py:26
  84.2 9.1 %all_to_all.49.found = f32[32,4,128]{2,1,0:T(4,128)S(1)} all-to-all(f32[32,4,128]{2,1,0:T(4,128)S(1)} %get-tuple-element.102), channel_id=1, replica_groups=mesh['tile'=16,'scene'=2] {'tile','scene'}, dimensions={0} | all-to-all | bytes 131072 | tf_op jit(solution)/shard_map/all_to_all | solution.py:1002
  93.4 3.0 %shard_map.283 = (bf16[32,48,128]{2,1,0:T(8,128)(2,1)S(1)}, f32[32]{0:T(128)}, f32[32]{0:T(128)}, f32[32]{0:T(128)}, f32[32]{0:T(128)}) custom-call(f32[32,4,128]{2,1,0:T(4,128)S(1)} %all_to_all.49.found, f32[128,8]{1,0:T(8,128)S(1)} %get-tuple-element.73.cols, f32[2,6,64,512]{3,2,1,0:T(8,128)S(1)} %get-tuple-element.103.grads, ...), custom_call_target="tpu_custom_call" | custom-call | tf_op jit(solution)/shard_map/pallas_call | solution.py:26
  96.3 14.9 %all_to_all.50.found = bf16[32,48,128]{2,1,0:T(8,128)(2,1)S(1)} all-to-all(bf16[32,48,128]{2,1,0:T(8,128)(2,1)S(1)} %get-tuple-element.109), channel_id=1, replica_groups=mesh['tile'=16,'scene'=2] {'tile','scene'}, dimensions={0} | all-to-all | bytes 786432 | tf_op jit(solution)/shard_map/all_to_all | solution.py:1002
  111.2 1.7 %shard_map.284 = (bf16[16,2,32,128]{3,2,1,0:T(8,128)(2,1)S(1)}, f32[2,64,4096]{2,1,0:T(8,128)S(1)}) custom-call(bf16[32,48,128]{2,1,0:T(8,128)(2,1)S(1)} %all_to_all.50.found, bf16[2,16,4096]{2,1,0:T(8,128)(2,1)S(1)} %copy-done.1, bf16[64,9]{1,0:T(8,128)(2,1)S(1)} %get-tuple-element.72.w_pillar, f32[128,8]{1,0:T(8,128)S(1)} %get-tuple-element.73.cols, ...), custom_call_target="tpu_custom_call" | custom-call | tf_op jit(solution)/shard_map/pallas_call | solution.py:26
  112.9 12.9 %all_to_all.51.found = bf16[32,32,128]{2,1,0:T(8,128)(2,1)S(1)} all-to-all(bf16[32,32,128]{2,1,0:T(8,128)(2,1)S(1)} %bitcast.15), channel_id=1, replica_groups=mesh['tile'=16,'scene'=2] {'tile','scene'}, dimensions={0} | all-to-all | bytes 524288 | tf_op jit(solution)/shard_map/all_to_all | solution.py:1002
  125.8 1.9 %shard_map.285 = (f32[2,1,9,32,128]{4,3,2,1,0:T(8,128)}, f32[9,32]{1,0:T(8,128)}, f32[32]{0:T(128)}, f32[32]{0:T(128)}, f32[32,576]{1,0:T(8,128)}, /*index=5*/f32[32,576]{1,0:T(8,128)}, f32[64,64]{1,0:T(8,128)}) custom-call(bf16[32,32,128]{2,1,0:T(8,128)(2,1)S(1)} %all_to_all.51.found, bf16[2,16,4096]{2,1,0:T(8,128)(2,1)S(1)} %copy-done.1, ...), custom_call_target="tpu_custom_call" | custom-call | tf_op jit(solution)/shard_map/pallas_call | solution.py:26
Async XLA Ops:
  3.1 14.7 %all-to-all-start = ((f32[32,4,128]{2,1,0:T(4,128)}), f32[32,4,128]{2,1,0:T(4,128)S(1)}, u32[]{:S(2)}, u32[]{:S(2)}) async-start(f32[32,4,128]{2,1,0:T(4,128)} %bitcast.16), calls=%async_computation | async-start | bytes 131072 | tf_op jit(solution)/shard_map/all_to_all | solution.py:1002
  12.5 14.8 %copy-start.1 = (bf16[2,16,4096]{2,1,0:T(8,128)(2,1)S(1)}, bf16[2,16,4096]{2,1,0:T(8,128)(2,1)}, u32[]{:S(2)}) copy-start(bf16[2,16,4096]{2,1,0:T(8,128)(2,1)} %get-tuple-element.70.point_rows.rows) | copy-start | bytes 786436
  17.9 1.0 copy-start
  21.7 13.1 %all-to-all-start.1 = ((bf16[16,16,384]{2,1,0:T(8,128)(2,1)}), bf16[16,16,384]{2,1,0:T(8,128)(2,1)S(1)}, u32[]{:S(2)}, u32[]{:S(2)}) async-start(bf16[16,16,384]{2,1,0:T(8,128)(2,1)} %bitcast.3), calls=%async_computation.1 | async-start | bytes 393216 | tf_op jit(solution)/shard_map/all_to_all | solution.py:1002
where the time goes:
time: 128 us
  blocking collectives  77.5 us (61%)
  Pallas kernels  27.4 us (21%)
  starting transfers between devices  11.5 us (9%)
  waiting for transfers between devices  8.17 us (6%)
  local copies, waits for them, and re-layouts  2.38 us (2%)
    all_to_all x7, blocking collectives, swap(): return lax.all_to_all(blocks, axes, split_axis=0, concat_axis=0)  75.2 us
    pallas_call x14, Pallas kernels, run(): pl.pallas_call(kernel, out_shape=[jax.ShapeDtypeStruct(out[0], out[1]) fo...  27.4 us
    all_to_all x2, starting transfers between devices, swap(): return lax.all_to_all(blocks, axes, split_axis=0, concat_axis=0)  11.5 us
    all_to_all x2, waiting for transfers between devices, swap(): return lax.all_to_all(blocks, axes, split_axis=0, concat_axis=0)  8.17 us
  transfers between devices with their start and end apart: 2, of which 2 were waited for; matrix products, arithmetic and copies ran while one was open for 1% of the time, Pallas kernels for 3%

commit v1 on v0

--- a/solution.py
+++ b/solution.py
@@ -322,7 +322,7 @@
 
 
 def pillar_kernel(
-    found, point_rows, w_pillar, cols, send, pooled, lifted, acts, *, capacity
+    found, point_rows, w_pillar, cols, send, pooled, lifted, acts, choices, *, capacity
 ):
     micros = point_rows.shape[0]
     channels, inputs = w_pillar.shape
@@ -332,9 +332,16 @@
     wide_weight = weight.astype(F32)
     rows_out = send.shape[0]
     square = inputs * inputs
-    stacked, slot_rows = [], []
-    for micro in range(micros):
-        lifted[...] = dot(weight, point_rows[micro, 0:inputs])
+    stacked = []
+    notes = [pillar_notes(point_rows, micro, inputs, pillars) for micro in range(micros)]
+    for micro in range(micros):
+        lifted[micro] = dot(weight, point_rows[micro, 0:inputs])
+    for group in range(3):
+        place = lax.broadcasted_iota(jnp.int32, (rows_out, pillars), 0) + (group - 1) * capacity
+        choices[group] = jnp.concatenate(
+            [jnp.where(place.astype(F32) == slot, 1.0, 0.0) for slot, _ in notes], axis=1
+        ).astype(BF16)
+    for micro in range(micros):
         moments = found[:, micro, :]
         sizes = moments[:, square + inputs : square + inputs + 1]
         means = moments[:, square : square + inputs]
@@ -367,12 +374,11 @@
         )
         scale = rstd * cols[0:channels, 0:1]
         shift = cols[0:channels, 1:2]
-        slot, limit = pillar_notes(point_rows, micro, inputs, pillars)
-        slot_rows.append(slot)
+        limit = notes[micro][1]
         top = jnp.full((channels, pillars), -jnp.inf, F32)
         for n in range(depth):
             piece = slice(n * pillars, (n + 1) * pillars)
-            normed = (lifted[:, piece] - centre) * scale + shift
+            normed = (lifted[micro, :, piece] - centre) * scale + shift
             act = normed * sigmoid(normed)
             acts[:, piece] = act
             top = jnp.maximum(top, jnp.where(limit > n, act, -jnp.inf))
@@ -387,11 +393,7 @@
         stacked.append(jnp.transpose(jnp.concatenate(parts, axis=0)))
     values = jnp.concatenate(stacked, axis=0).astype(BF16)
     for group in range(3):
-        place = lax.broadcasted_iota(jnp.int32, (rows_out, pillars), 0) + (group - 1) * capacity
-        chosen = jnp.concatenate(
-            [jnp.where(place.astype(F32) == row, 1.0, 0.0) for row in slot_rows], axis=1
-        ).astype(BF16)
-        send[:, group * LANES : (group + 1) * LANES] = dot(chosen, values).astype(BF16)
+        send[:, group * LANES : (group + 1) * LANES] = dot(choices[group], values).astype(BF16)
 
 
 def own_stats(ref, first_row, rows, send):
@@ -780,9 +782,17 @@
     found, cols, grads, first_out, first_stats, b_first_in, where_rows,
     canvas, second_grad, top_grad, expected,
     send, gain_grad, shift_grad, second_gain_grad, second_shift_grad, low, grid, b_first, first_grad, whole,
+    choices,
     *, rows, tiles, each
 ):
     expand(b_first_in, b_first)
+    columns = jnp.transpose(where_rows[...])
+    slots, width = columns.shape[0], grads.shape[3]
+    lane = lax.broadcasted_iota(jnp.int32, (slots, width), 1).astype(F32)
+    for at in range(choices.shape[0]):
+        column = columns[:, at : at + 1] - 1.0
+        column = column - jnp.floor(column * (1.0 / width)) * width
+        choices[at] = jnp.where(lane == column, 1.0, 0.0).astype(BF16)
     scene = lax.axis_index("scene")
     micros, high, channels, width = grads.shape
     sums = sum_rows(found, 2 + micros)
@@ -825,20 +835,14 @@
         whole[s, 0 : parts.shape[0]] = parts
         if whole.shape[1] > parts.shape[0]:
             whole[s, parts.shape[0] :] = jnp.zeros((whole.shape[1] - parts.shape[0], LANES), F32)
-    columns = jnp.transpose(where_rows[...])
-    slots = columns.shape[0]
-    lane = lax.broadcasted_iota(jnp.int32, (slots, width), 1).astype(F32)
     groups = []
     for group in range(3):
         start, first, count = ((0, rows - 2, 2), (2, 0, rows), (rows + 2, 0, 2))[group]
         picked = []
         for micro in range(micros):
             at = 2 * group + micro
-            column = columns[:, at : at + 1] - 1.0
-            column = column - jnp.floor(column * (1.0 / width)) * width
-            chosen = jnp.where(lane == column, 1.0, 0.0).astype(BF16)
             place = jnp.floor((where_rows[at : at + 1] - 1.0) * (1.0 / width))
-            here = dot_lanes(grid[micro, start : start + count].reshape(count * channels, width), chosen)
+            here = dot_lanes(grid[micro, start : start + count].reshape(count * channels, width), choices[at])
             total = jnp.zeros((channels, slots), F32)
             for r in range(count):
                 total = total + jnp.where(
@@ -880,7 +884,7 @@
             out[micro, :, piece] = jnp.where(limit > n, jnp.exp(act - pool) * slope, 0.0).astype(BF16)
 
 
-def pillar_back_kernel(found, rows, w_pillar, cols, pooled, factors, send, grads, lifted, *, capacity, each):
+def pillar_back_kernel(found, rows, w_pillar, cols, pooled, factors, send, grads, lifted, choices, *, capacity, each):
     micros = rows.shape[0]
     _, channels, pillars = pooled.shape
     stats = pooled.at[micros : 2 * micros]
@@ -889,6 +893,11 @@
     scene = lax.axis_index("scene")
     peers = found.shape[0]
     slot_count = peers // 2 * capacity
+    place = lax.broadcasted_iota(jnp.int32, (slot_count, pillars), 0).astype(F32)
+    for micro in range(micros):
+        lifted[micro] = dot(w_pillar[...], rows[micro, 0:inputs])
+        slot, _ = pillar_notes(rows, micro, inputs, pillars)
+        choices[micro] = jnp.where(place == slot, 1.0, 0.0).astype(BF16)
     blocks = [found[2 * t + scene].astype(F32) for t in range(peers // 2)]
     before, own, after = [
         jnp.concatenate([block[group * capacity : (group + 1) * capacity] for block in blocks], axis=0)
@@ -901,15 +910,11 @@
         + jnp.concatenate([gap, after[: slot_count - capacity]], axis=0)
     )
     turned = jnp.transpose(returned)
-    place = lax.broadcasted_iota(jnp.int32, (slot_count, pillars), 0).astype(F32)
     gain = cols[0:channels, 0:1]
     gain_sums, shift_sums = [], []
     outer = jnp.zeros((16, channels), F32)
     for micro in range(micros):
-        lifted[...] = dot(w_pillar[...], rows[micro, 0:inputs])
-        slot, _ = pillar_notes(rows, micro, inputs, pillars)
-        chosen = jnp.where(place == slot, 1.0, 0.0).astype(BF16)
-        back = dot(turned[micro * channels : (micro + 1) * channels].astype(BF16), chosen)
+        back = dot(turned[micro * channels : (micro + 1) * channels].astype(BF16), choices[micro])
         centre, rstd = stats[micro, :, 0:1], stats[micro, :, 1:2]
         gain_sum = jnp.zeros((channels, pillars), F32)
         shift_sum = jnp.zeros((channels, pillars), F32)
@@ -917,7 +922,7 @@
             piece = slice(n * pillars, (n + 1) * pillars)
             grad = back * factors[micro, :, piece].astype(F32)
             grads[micro, :, piece] = grad
-            gain_sum = gain_sum + grad * (lifted[:, piece] - centre)
+            gain_sum = gain_sum + grad * (lifted[micro, :, piece] - centre)
             shift_sum = shift_sum + grad
         gain_sum = gain_sum * rstd
         gain_sums.append(gain_sum)
@@ -947,6 +952,8 @@
     stats = pooled.at[micros : 2 * micros]
     _, _, inputs, depth, pillars = points_grad.shape
     half = channels // 2
+    for micro in range(micros):
+        lifted[micro] = dot(w_pillar[...], rows[micro, 0:inputs])
     total = jnp.sum(found[...].astype(F32), axis=0)
     total = jnp.concatenate([total[0:2] + total[2:4], total[4:9]], axis=0)
     own_half(total[0:1, :channels] + total[0:1, channels:], scene, gain_grad)
@@ -958,7 +965,6 @@
     )
     weight = jnp.transpose(w_pillar[...].astype(F32)).astype(BF16)
     for micro in range(micros):
-        lifted[...] = dot(w_pillar[...], rows[micro, 0:inputs])
         part = slice(micro * channels, (micro + 1) * channels)
         centre, rstd, inverse = stats[micro, :, 0:1], stats[micro, :, 1:2], stats[micro, :, 2:3]
         factor = cols[0:channels, 0:1] * rstd
@@ -969,7 +975,7 @@
         _, limit = pillar_notes(rows, micro, inputs, pillars)
         for n in range(depth):
             piece = slice(n * pillars, (n + 1) * pillars)
-            low = factor * (grads[micro, :, piece] - shift_part - (lifted[:, piece] - centre) * gain_part)
+            low = factor * (grads[micro, :, piece] - shift_part - (lifted[micro, :, piece] - centre) * gain_part)
             low = jnp.where(limit > n, low, 0.0).astype(BF16)
             points_grad[micro, 0, :, n, :] = dot(weight, low)
     weight_grad = jnp.concatenate([weight_grad, jnp.zeros((channels, LANES - inputs), F32)], axis=1)
@@ -1067,7 +1073,10 @@
         functools.partial(pillar_kernel, capacity=capacity),
         [((slot_count, 3 * LANES), BF16), ((2 * micros, channels, pillars), F32)],
         moments, point_rows, w_pillar, cols,
-        scratch=[vmem((channels, depth * pillars), F32), vmem((channels, depth * pillars), F32)],
+        scratch=[
+            vmem((micros, channels, depth * pillars), F32), vmem((channels, depth * pillars), F32),
+            vmem((3, slot_count, micros * pillars), BF16),
+        ],
     )
     arrived = swap(send.reshape(tiles, capacity, 3 * LANES), "tile").reshape(slot_count, 3 * LANES)
     (cell_rows,) = run(
@@ -1141,7 +1150,7 @@
         canvas, second_cross, top_grad, expected,
         scratch=[
             vmem(*grid(rows + 2, BF16, 3 * channels)), vmem(*grid(rows + 4, BF16)), vmem(*taps), vmem(*cross),
-            vmem((scenes, tiles * each, LANES), F32),
+            vmem((scenes, tiles * each, LANES), F32), vmem((3 * micros, slot_count, width), BF16),
         ],
     )
     block = -(-(9 + each) // 8) * 8
@@ -1149,7 +1158,9 @@
         functools.partial(pillar_back_kernel, capacity=capacity, each=each),
         [((tiles, scenes, block, LANES), BF16), ((micros, channels, depth * pillars), F32)],
         swap(send, BOTH), point_rows, w_pillar, cols, pooled, factors,
-        scratch=[vmem((channels, depth * pillars), F32)],
+        scratch=[
+            vmem((micros, channels, depth * pillars), F32), vmem((micros, slot_count, pillars), BF16),
+        ],
     )
     points_grad, pillar_grad, pillar_gain_grad, pillar_shift_grad, first_grad, second_grad, up_grad = run(
         functools.partial(points_kernel, each=each),
@@ -1158,7 +1169,7 @@
             matrix, matrix, ((upper // 2, channels), F32),
         ],
         swap(send.reshape(peers, block, LANES), BOTH), point_rows, pillar_dz, w_pillar, cols, pooled,
-        scratch=[vmem((channels, depth * pillars), F32)],
+        scratch=[vmem((micros, channels, depth * pillars), F32)],
     )
     return (
         features, points_grad,

time: 128 us -> 128 us (level)
  no operation moved by 1% of the time
where the time goes in v1:
time: 128 us; the launch traced here: 127 us
  blocking collectives  77.5 us (61%)
  Pallas kernels  27 us (21%)
  starting transfers between devices  11.5 us (9%)
  waiting for transfers between devices  8.17 us (6%)
  local copies, waits for them, and re-layouts  2.38 us (2%)
    all_to_all x7, blocking collectives, swap(): return lax.all_to_all(blocks, axes, split_axis=0, concat_axis=0)  75.2 us
    pallas_call x14, Pallas kernels, run(): pl.pallas_call(kernel, out_shape=[jax.ShapeDtypeStruct(out[0], out[1]) fo...  27 us
    all_to_all x2, starting transfers between devices, swap(): return lax.all_to_all(blocks, axes, split_axis=0, concat_axis=0)  11.5 us
    all_to_all x2, waiting for transfers between devices, swap(): return lax.all_to_all(blocks, axes, split_axis=0, concat_axis=0)  8.17 us
  transfers between devices with their start and end apart: 2, of which 2 were waited for; matrix products, arithmetic and copies ran while one was open for 1% of the time, Pallas kernels for 3%

profile of v1, /device:TPU:0, one launch (start us, length us, event | category | flops | bytes accessed | tf_op | source)
XLA Modules:
  0.0 127.2 jit_solution(16148371104927796258)
XLA Ops:
  0.6 2.5 %shard_map.272 = f32[16,2,4,128]{3,2,1,0:T(4,128)} custom-call(s32[2,1,128]{2,1,0:T(1,128)} %refs_0_.3, s32[2,1,128]{2,1,0:T(1,128)} %refs_1_.2, s32[2,1,128]{2,1,0:T(1,128)} %refs_1_.3, bf16[2,1,9,32,128]{4,3,2,1,0:T(8,128)(2,1)} %refs_2_.3), custom_call_target="tpu_custom_call" | custom-call | tf_op jit(solution)/shard_map/pallas_call | solution.py:26
  3.1 7.3 %all-to-all-start = ((f32[32,4,128]{2,1,0:T(4,128)}), f32[32,4,128]{2,1,0:T(4,128)S(1)}, u32[]{:S(2)}, u32[]{:S(2)}) async-start(f32[32,4,128]{2,1,0:T(4,128)} %bitcast.16), calls=%async_computation | async-start | bytes 131072 | tf_op jit(solution)/shard_map/all_to_all | solution.py:1008
  10.5 2.0 %shard_map.273 = (bf16[416,128]{1,0:T(8,128)(2,1)}, bf16[2,16,4096]{2,1,0:T(8,128)(2,1)}) custom-call(s32[2,1,128]{2,1,0:T(1,128)} %refs_0_.3, s32[2,1,128]{2,1,0:T(1,128)} %refs_1_.3, bf16[2,1,9,32,128]{4,3,2,1,0:T(8,128)(2,1)} %refs_2_.3, bf16[32,576]{1,0:T(8,128)(2,1)} %refs_3_.3, bf16[32,576]{1,0:T(8,128)(2,1)} %refs_4_.1, bf16[64,64]{1,0:T(8,128)(2,1)} %refs_5_.1, ...), custom_call_target="tpu_custom_call" | custom-call | flops 10000000 | bytes 1000000 | tf_op jit(solution)/shard_map/pallas_call | solution.py:26
  12.5 0.0 copy-start.1
  12.5 2.3 %all-gather = bf16[832,128]{1,0:T(8,128)(2,1)S(1)} all-gather(bf16[416,128]{1,0:T(8,128)(2,1)} %get-tuple-element.71), channel_id=2, replica_groups=mesh['tile'=16,'scene'=2] {'scene'}, dimensions={0}, use_global_device_ids=true | all-gather | bytes 319488 | tf_op jit(solution)/shard_map/all_gather | solution.py:1059
  14.8 0.4 shard_map.274
  15.2 2.7 %all-to-all-done.found = f32[32,4,128]{2,1,0:T(4,128)S(1)} async-done(((f32[32,4,128]{2,1,0:T(4,128)}), f32[32,4,128]{2,1,0:T(4,128)S(1)}, u32[]{:S(2)}, u32[]{:S(2)}) %all-to-all-start) | async-done | bytes 65568 | tf_op jit(solution)/shard_map/all_to_all | solution.py:1008
  17.9 0.0 copy-start
  17.9 0.9 copy-done
  18.8 2.8 %shard_map.275 = (bf16[256,384]{1,0:T(8,128)(2,1)}, f32[4,64,128]{2,1,0:T(8,128)S(1)}) custom-call(f32[32,4,128]{2,1,0:T(4,128)S(1)} %all-to-all-done.found, bf16[2,16,4096]{2,1,0:T(8,128)(2,1)S(1)} %copy-done, bf16[64,9]{1,0:T(8,128)(2,1)S(1)} %get-tuple-element.72.w_pillar, f32[128,8]{1,0:T(8,128)S(1)} %get-tuple-element.73.cols), custom_call_target="tpu_custom_call" | custom-call | tf_op jit(solution)/shard_map/pallas_call | solution.py:26
  21.6 4.2 %all-to-all-start.1 = ((bf16[16,16,384]{2,1,0:T(8,128)(2,1)}), bf16[16,16,384]{2,1,0:T(8,128)(2,1)S(1)}, u32[]{:S(2)}, u32[]{:S(2)}) async-start(bf16[16,16,384]{2,1,0:T(8,128)(2,1)} %bitcast.3), calls=%async_computation.1 | async-start | bytes 393216 | tf_op jit(solution)/shard_map/all_to_all | solution.py:1008
  25.8 1.4 %copy.33 = bf16[2,1,128,4,512]{4,2,3,0,1:T(8,128)(2,1)S(1)} copy(bf16[2,1,128,4,512]{4,3,2,1,0:T(4,128)(2,1)} %param.33) | data formatting | bytes 2097152 | tf_op args[16]
  27.2 0.0 copy-done.1
  27.2 1.5 %shard_map.276.factors = bf16[2,64,4096]{2,1,0:T(8,128)(2,1)S(1)} custom-call(bf16[2,16,4096]{2,1,0:T(8,128)(2,1)S(1)} %copy-done.1, bf16[64,9]{1,0:T(8,128)(2,1)S(1)} %get-tuple-element.72.w_pillar, f32[128,8]{1,0:T(8,128)S(1)} %get-tuple-element.73.cols, f32[4,64,128]{2,1,0:T(8,128)S(1)} %get-tuple-element.75.pooled), custom_call_target="tpu_custom_call" | custom-call | flops 10000000 | bytes 1000000 | tf_op jit(solution)/shard_map/pallas_call | solution.py:26
  28.7 0.5 shard_map.277.where_rows
  29.3 5.5 %all-to-all-done.1 = bf16[16,16,384]{2,1,0:T(8,128)(2,1)S(1)} async-done(((bf16[16,16,384]{2,1,0:T(8,128)(2,1)}), bf16[16,16,384]{2,1,0:T(8,128)(2,1)S(1)}, u32[]{:S(2)}, u32[]{:S(2)}) %all-to-all-start.1) | async-done | bytes 196640 | tf_op jit(solution)/shard_map/all_to_all | solution.py:1008
  34.8 1.5 %shard_map.278 = (f32[2,6,64,512]{3,2,1,0:T(8,128)S(1)}, bf16[2,8,64,512]{3,2,1,0:T(8,128)(2,1)S(1)}, f32[32,2,128]{2,1,0:T(2,128)S(1)}) custom-call(bf16[256,384]{1,0:T(8,128)(2,1)S(1)} %bitcast.14, f32[8,256]{1,0:T(8,128)S(1)} %shard_map.277.where_rows, bf16[64,576]{1,0:T(8,128)(2,1)S(1)} %get-tuple-element.77.l_first_in), custom_call_target="tpu_custom_call" | custom-call | tf_op jit(solution)/shard_map/pallas_call | solution.py:26
  36.3 9.4 %all_to_all.45.found = f32[32,2,128]{2,1,0:T(2,128)S(1)} all-to-all(f32[32,2,128]{2,1,0:T(2,128)S(1)} %get-tuple-element.78), channel_id=1, replica_groups=mesh['tile'=16,'scene'=2] {'tile','scene'}, dimensions={0} | all-to-all | bytes 65536 | tf_op jit(solution)/shard_map/all_to_all | solution.py:1008
  45.7 1.6 %shard_map.279 = (f32[2,4,64,512]{3,2,1,0:T(8,128)S(1)}, bf16[2,6,64,512]{3,2,1,0:T(8,128)(2,1)S(1)}, f32[2,6,64,512]{3,2,1,0:T(8,128)S(1)}, f32[128,8]{1,0:T(8,128)S(1)}, f32[32,2,128]{2,1,0:T(2,128)S(1)}) custom-call(f32[32,2,128]{2,1,0:T(2,128)S(1)} %all_to_all.45.found, f32[128,8]{1,0:T(8,128)S(1)} %get-tuple-element.73.cols, ...), custom_call_target="tpu_custom_call" | custom-call | tf_op jit(solution)/shard_map/pallas_call | solution.py:26
  47.3 8.9 %all_to_all.46.found = f32[32,2,128]{2,1,0:T(2,128)S(1)} all-to-all(f32[32,2,128]{2,1,0:T(2,128)S(1)} %get-tuple-element.81), channel_id=1, replica_groups=mesh['tile'=16,'scene'=2] {'tile','scene'}, dimensions={0} | all-to-all | bytes 65536 | tf_op jit(solution)/shard_map/all_to_all | solution.py:1008
  56.2 1.6 %shard_map.280 = (bf16[2,4,64,512]{3,2,1,0:T(8,128)(2,1)S(1)}, f32[2,4,128,512]{3,2,1,0:T(8,128)S(1)}, f32[2,4,128,512]{3,2,1,0:T(8,128)S(1)}, f32[2,128]{1,0:T(...) custom-call(f32[32,2,128]{2,1,0:T(2,128)S(1)} %all_to_all.46.found, ...), custom_call_target="tpu_custom_call" | custom-call | tf_op jit(solution)/shard_map/pallas_call | solution.py:26
  57.8 9.9 %all_to_all.47.found = f32[32,8,128]{2,1,0:T(8,128)S(1)} all-to-all(f32[32,8,128]{2,1,0:T(8,128)S(1)} %get-tuple-element.84), channel_id=1, replica_groups=mesh['tile'=16,'scene'=2] {'tile','scene'}, dimensions={0} | all-to-all | bytes 262144 | tf_op jit(solution)/shard_map/all_to_all | solution.py:1008
  67.8 2.8 %shard_map.281 = (bf16[2,1,128,4,512]{4,3,2,1,0:T(4,128)(2,1)}, f32[2,4,128,512]{3,2,1,0:T(8,128)S(1)}, f32[2,128]{1,0:T(2,128)S(1)}, f32[128,8]{1,0:T(8,128)S(1)}, bf16[32,16,128]{2,1,0:T(8,128)(2,1)S(1)}) custom-call(f32[32,8,128]{2,1,0:T(8,128)S(1)} %all_to_all.47.found, f32[128,8]{1,0:T(8,128)S(1)} %get-tuple-element.73.cols, ...), custom_call_target="tpu_custom_call" | custom-call | tf_op jit(solution)/shard_map/pallas_call | solution.py:26
  70.6 9.9 %all_to_all.48.found = bf16[32,16,128]{2,1,0:T(8,128)(2,1)S(1)} all-to-all(bf16[32,16,128]{2,1,0:T(8,128)(2,1)S(1)} %get-tuple-element.91), channel_id=1, replica_groups=mesh['tile'=16,'scene'=2] {'tile','scene'}, dimensions={0} | all-to-all | bytes 262144 | tf_op jit(solution)/shard_map/all_to_all | solution.py:1008
  80.5 3.7 %shard_map.282 = (f32[2,6,64,512]{3,2,1,0:T(8,128)S(1)}, f32[128,64]{1,0:T(8,128)S(1)}, f32[192,192]{1,0:T(8,128)S(1)}, f32[64]{0:T(128)}, f32[64]{0:T(128)}, /*...) custom-call(bf16[32,16,128]{2,1,0:T(8,128)(2,1)S(1)} %all_to_all.48.found, f32[128,8]{1,0:T(8,128)S(1)} %get-tuple-element.73.cols, ...), custom_call_target="tpu_custom_call" | custom-call | tf_op jit(solution)/shard_map/pallas_call | solution.py:26
  84.2 9.2 %all_to_all.49.found = f32[32,4,128]{2,1,0:T(4,128)S(1)} all-to-all(f32[32,4,128]{2,1,0:T(4,128)S(1)} %get-tuple-element.102), channel_id=1, replica_groups=mesh['tile'=16,'scene'=2] {'tile','scene'}, dimensions={0} | all-to-all | bytes 131072 | tf_op jit(solution)/shard_map/all_to_all | solution.py:1008
  93.3 3.0 %shard_map.283 = (bf16[32,48,128]{2,1,0:T(8,128)(2,1)S(1)}, f32[32]{0:T(128)}, f32[32]{0:T(128)}, f32[32]{0:T(128)}, f32[32]{0:T(128)}) custom-call(f32[32,4,128]{2,1,0:T(4,128)S(1)} %all_to_all.49.found, f32[128,8]{1,0:T(8,128)S(1)} %get-tuple-element.73.cols, f32[2,6,64,512]{3,2,1,0:T(8,128)S(1)} %get-tuple-element.103.grads, ...), custom_call_target="tpu_custom_call" | custom-call | tf_op jit(solution)/shard_map/pallas_call | solution.py:26
  96.3 14.9 %all_to_all.50.found = bf16[32,48,128]{2,1,0:T(8,128)(2,1)S(1)} all-to-all(bf16[32,48,128]{2,1,0:T(8,128)(2,1)S(1)} %get-tuple-element.109), channel_id=1, replica_groups=mesh['tile'=16,'scene'=2] {'tile','scene'}, dimensions={0} | all-to-all | bytes 786432 | tf_op jit(solution)/shard_map/all_to_all | solution.py:1008
  111.2 1.3 %shard_map.284 = (bf16[16,2,32,128]{3,2,1,0:T(8,128)(2,1)S(1)}, f32[2,64,4096]{2,1,0:T(8,128)S(1)}) custom-call(bf16[32,48,128]{2,1,0:T(8,128)(2,1)S(1)} %all_to_all.50.found, bf16[2,16,4096]{2,1,0:T(8,128)(2,1)S(1)} %copy-done.1, bf16[64,9]{1,0:T(8,128)(2,1)S(1)} %get-tuple-element.72.w_pillar, f32[128,8]{1,0:T(8,128)S(1)} %get-tuple-element.73.cols, ...), custom_call_target="tpu_custom_call" | custom-call | tf_op jit(solution)/shard_map/pallas_call | solution.py:26
  112.5 12.9 %all_to_all.51.found = bf16[32,32,128]{2,1,0:T(8,128)(2,1)S(1)} all-to-all(bf16[32,32,128]{2,1,0:T(8,128)(2,1)S(1)} %bitcast.15), channel_id=1, replica_groups=mesh['tile'=16,'scene'=2] {'tile','scene'}, dimensions={0} | all-to-all | bytes 524288 | tf_op jit(solution)/shard_map/all_to_all | solution.py:1008
  125.4 1.8 %shard_map.285 = (f32[2,1,9,32,128]{4,3,2,1,0:T(8,128)}, f32[9,32]{1,0:T(8,128)}, f32[32]{0:T(128)}, f32[32]{0:T(128)}, f32[32,576]{1,0:T(8,128)}, /*index=5*/f32[32,576]{1,0:T(8,128)}, f32[64,64]{1,0:T(8,128)}) custom-call(bf16[32,32,128]{2,1,0:T(8,128)(2,1)S(1)} %all_to_all.51.found, bf16[2,16,4096]{2,1,0:T(8,128)(2,1)S(1)} %copy-done.1, ...), custom_call_target="tpu_custom_call" | custom-call | tf_op jit(solution)/shard_map/pallas_call | solution.py:26
Async XLA Ops:
  3.1 14.7 %all-to-all-start = ((f32[32,4,128]{2,1,0:T(4,128)}), f32[32,4,128]{2,1,0:T(4,128)S(1)}, u32[]{:S(2)}, u32[]{:S(2)}) async-start(f32[32,4,128]{2,1,0:T(4,128)} %bitcast.16), calls=%async_computation | async-start | bytes 131072 | tf_op jit(solution)/shard_map/all_to_all | solution.py:1008
  12.5 14.7 %copy-start.1 = (bf16[2,16,4096]{2,1,0:T(8,128)(2,1)S(1)}, bf16[2,16,4096]{2,1,0:T(8,128)(2,1)}, u32[]{:S(2)}) copy-start(bf16[2,16,4096]{2,1,0:T(8,128)(2,1)} %get-tuple-element.70.point_rows.rows) | copy-start | bytes 786436
  17.9 1.0 copy-start
  21.6 13.1 %all-to-all-start.1 = ((bf16[16,16,384]{2,1,0:T(8,128)(2,1)}), bf16[16,16,384]{2,1,0:T(8,128)(2,1)S(1)}, u32[]{:S(2)}, u32[]{:S(2)}) async-start(bf16[16,16,384]{2,1,0:T(8,128)(2,1)} %bitcast.3), calls=%async_computation.1 | async-start | bytes 393216 | tf_op jit(solution)/shard_map/all_to_all | solution.py:1008
